TPU v7x, 128 devices: a whole 4x4x4 slice. The times are simulated.
128 devices in a mesh: chain: 16 (over z, y), sector: 8 (over x, core).
Axes of the slice: x: 4, y: 4, z: 4, core: 2. Of those that a mesh axis runs over, the one named last changes fastest.
Arguments:
- theta: bfloat16 [16, 16, 16, 256, 256], P('chain', 'sector'), may hold values from -6 to 6
- env_left0: bfloat16 [16, 2, 256, 256], P('sector'), may hold values from -0.375 to 0.375
- transfer: float32 [16, 16, 256, 256], P('chain', 'sector')
- env_right: bfloat16 [16, 16, 2, 256, 256], P('chain', 'sector'), may hold values from -0.375 to 0.375
- mpo_weights: float32 [2, 16, 16], replicated, may hold values from -1.5 to 1.5
- term_mask: int32 [16, 2], P('sector'), may hold values 0 or 1
- block_sizes: int32 [16], P('sector'), may hold values from 64 to 256, as said below
- ritz: float32 [16, 4], P('chain'), may hold values from -4 to 4
Outputs:
- psi: float32 [16, 16, 16, 256, 256], P('chain', 'sector')
- tridiag: float32 [16, 2, 3], P('chain')
Inputs may be any that keep to these rules, and one draw needn't show every extreme that they name: `block_sizes`: each size lies between 64 and 256; both ends occur in every draw.
All inputs are finite; a program needn't handle non-finite values. No bound on the sum of `term_mask` on one device may be relied on, other than what follows from the above.
Results may differ from a plain program's by a relative error of at most 0.0075.
Values may be sent and summed in bfloat16 or wider, within the bound.
A program may use at most 192 MiB of HBM per device.

v0:
```python
import jax
import jax.numpy as jnp
import numpy as np
from jax import lax
from jax.sharding import PartitionSpec as P

charge_table = np.array([-2, -1, -1, -1, -1, 0, 0, 0, 0, 0, 0, 1, 1, 1, 1, 2])
group_bounds = [(0, 1), (1, 5), (5, 11), (11, 15), (15, 16)]
highest = lax.Precision.HIGHEST
eps = 1e-06


def from_behind(block, axis, distance):
    devices = range(lax.axis_size(axis))
    route = [(i - distance, i) for i in devices if i - distance in devices]
    return lax.ppermute(block, axis, route)


def extended(cells, sides, width):
    for axis, dim in sides:
        count = lax.axis_size(axis)
        ends = count - 1
        head = lax.slice_in_dim(cells, 0, width, axis=dim)
        tail = lax.slice_in_dim(cells, cells.shape[dim] - width, cells.shape[dim], axis=dim)
        cells = jnp.concatenate(
            [
                lax.ppermute(tail, axis, [(i, (i + 1) % count) for i in range(ends)]),
                cells,
                lax.ppermute(head, axis, [((i + 1) % count, i) for i in range(ends)]),
            ],
            axis=dim,
        )
    return cells


def chain_product(earlier, later):
    return jnp.einsum("sij,sjk->sik", earlier, later, precision=highest)


def apply_operator(vector, left_env, right_pad, mixing, gates):
    total = jnp.zeros(vector.shape, jnp.float32)
    count_sec = vector.shape[0]
    for term in range(mixing.shape[0]):
        mixed = jnp.einsum("pq,sqij->spij", mixing[term], vector, precision=highest).astype(
            jnp.bfloat16
        )
        upper = jnp.einsum(
            "sik,spkj->spij", left_env[:, term], mixed, preferred_element_type=jnp.float32
        ).astype(jnp.bfloat16)
        pieces = []
        for level in range(5):
            begin, finish = group_bounds[level]
            picked = right_pad[level : level + count_sec, term]
            pieces.append(
                jnp.einsum(
                    "spij,slj->spil",
                    upper[:, begin:finish],
                    picked,
                    preferred_element_type=jnp.float32,
                )
            )
        joined = jnp.concatenate(pieces, axis=1)
        total = total + gates[:, term][:, None, None, None] * joined
    return total


def on_device(theta, env_left0, transfer, env_right, mpo_weights, term_mask, block_sizes, ritz):
    width = theta.shape[-1]
    live = (jnp.arange(width)[None, :] < block_sizes[:, None]).astype(jnp.float32)
    box_mask = live[:, :, None] * live[:, None, :]
    same = (charge_table[:, None] == charge_table[None, :]).astype(np.float32)
    mixing = mpo_weights * jnp.asarray(same, jnp.float32)
    gates = term_mask.astype(jnp.float32)
    factor = transfer[0] * box_mask
    identity = jnp.broadcast_to(jnp.eye(width, dtype=jnp.float32), factor.shape)
    below = from_behind(factor, "chain", 1)
    at_start = lax.axis_index("chain") == 0

    def relay_step(turn, held):
        incoming = from_behind(held, "chain", 1)
        built = chain_product(incoming, below)
        return jnp.where(at_start, identity, built)

    prefix = lax.fori_loop(0, lax.axis_size("chain") - 1, relay_step, identity)
    left_base = env_left0.astype(jnp.float32) * box_mask[:, None]
    inner = jnp.einsum("swjk,skl->swjl", left_base, prefix, precision=highest)
    left_env = jnp.einsum("sji,swjl->swil", prefix, inner, precision=highest).astype(jnp.bfloat16)
    right_env = env_right[0] * box_mask[:, None].astype(jnp.bfloat16)
    right_pad = extended(right_env, (("sector", 0),), 2)
    count = float(theta.shape[1] * lax.axis_size("sector") * theta.shape[2] * width * width)
    start = theta[0].astype(jnp.float32) * box_mask[:, None]
    start_sq = lax.psum(jnp.sum(start * start), "sector")
    vectors = [start / jnp.sqrt(start_sq / count + eps)]
    alphas = []
    betas = []
    for step in range(ritz.shape[1] - 1):
        current = vectors[-1]
        image = apply_operator(current, left_env, right_pad, mixing, gates)
        previous = vectors[-2] if step > 0 else jnp.zeros_like(current)
        beta_prev = betas[-1] if step > 0 else jnp.float32(0.0)
        alpha = lax.psum(jnp.sum(current * image), "sector") / count
        image = image - alpha * current - beta_prev * previous
        beta = jnp.sqrt(lax.psum(jnp.sum(image * image), "sector") / count + eps)
        vectors.append(image / beta)
        alphas.append(alpha)
        betas.append(beta)
    combined = jnp.zeros(start.shape, jnp.float32)
    for index in range(ritz.shape[1]):
        combined = combined + ritz[0, index] * vectors[index]
    tridiag = jnp.stack([jnp.stack(alphas), jnp.stack(betas)])
    return (combined[None], tridiag[None])


def solution(mesh):
    in_specs = (
        P("chain", "sector", None, None, None),
        P("sector", None, None, None),
        P("chain", "sector", None, None),
        P("chain", "sector", None, None, None),
        P(),
        P("sector", None),
        P("sector"),
        P("chain", None),
    )
    out_specs = (P("chain", "sector", None, None, None), P("chain", None, None))
    return jax.shard_map(
        on_device, mesh=mesh, in_specs=in_specs, out_specs=out_specs, check_vma=False
    )
```

profile of v0, /device:TPU:97, one launch (start us, length us, event | category | flops | bytes accessed | tf_op | source)
XLA Modules:
  0.0 711.4 jit_solution(1506947315203285644)
XLA Ops:
  3.6 3.7 collective-permute-start.2
  9.3 3.2 collective-permute-start.1
  12.5 5.0 fusion.6
  17.5 13.5 %psum.49 = f32[]{:T(128)} all-reduce(f32[]{:T(128)} %fusion.6), channel_id=1, replica_groups=mesh['chain'=16,'sector'=8] {'sector'}, use_global_device_ids=true, to_apply=%region_1.2 | all-reduce | flops 1 | bytes 8 | tf_op jit(solution)/shard_map/psum | solution.py:92
  31.7 3.3 fusion.77
  35.0 3.4 copy-done.4
  38.4 11.9 %fusion.15 = bf16[2,256,256,16]{2,3,1,0:T(8,128)(2,1)} fusion(f32[2,16,256,256]{3,2,1,0:T(8,128)S(1)} %fusion.77, f32[2,16,16]{2,1,0:T(8,128)S(1)} %broadcast_multiply_fusion.1), kind=kOutput, calls=%fused_computation.31 | convolution fusion | flops 402653184 | bytes 12591104 | tf_op jit(solution)/shard_map/pq,sqij->spij/dot_general | solution.py:44
  50.3 7.5 %copy.64 = bf16[2,256,256,16]{1,2,3,0:T(8,128)(2,1)} copy(bf16[2,256,256,16]{2,3,1,0:T(8,128)(2,1)} %fusion.15) | data formatting | bytes 8388608 | tf_op jit(solution)/shard_map/pq,sqij->spij/dot_general | solution.py:44
  57.8 16.5 %fusion.17 = bf16[2,256,256,16]{2,3,1,0:T(8,128)(2,1)} fusion(f32[2,16,256,256]{3,2,1,0:T(8,128)} %copy-done.4, f32[2,16,16]{2,1,0:T(8,128)S(1)} %broadcast_multiply_fusion.1), kind=kOutput, calls=%fused_computation.33 | convolution fusion | flops 402653184 | bytes 12591104 | tf_op jit(solution)/shard_map/pq,sqij->spij/dot_general | solution.py:44
  74.3 7.5 %copy.52 = bf16[2,256,256,16]{1,2,3,0:T(8,128)(2,1)} copy(bf16[2,256,256,16]{2,3,1,0:T(8,128)(2,1)} %fusion.17) | data formatting | bytes 8388608 | tf_op jit(solution)/shard_map/pq,sqij->spij/dot_general | solution.py:44
  82.9 241.0 %while.11 = (s32[]{:T(128)}, f32[2,256,256]{2,1,0:T(8,128)}, pred[]{:T(512)}, f32[2,256,256]{2,1,0:T(8,128)S(1)}, f32[256,256]{1,0:T(8,128)S(1)}, /*index=5*/s32[]{:T(128)}) while((s32[]{:T(128)}, f32[2,256,256]{2,1,0:T(8,128)}, pred[]{:T(512)}, f32[2,256,256]{2,1,0:T(8,128)S(1)}, f32[256,256]{1,0:T(8,128)S(1)}, ...), condition=%wide.region_3.4_spmd.clone, body=%wide.region_2.3_spmd.clone.sunk | while | flops 402784256 | bytes 3932270 | solution.py:84
  82.9 2.9 collective-permute-start
  85.8 13.1 %collective-permute-done = f32[2,256,256]{2,1,0:T(8,128)S(1)} collective-permute-done((f32[2,256,256]{2,1,0:T(8,128)}, f32[2,256,256]{2,1,0:T(8,128)S(1)}, u32[]{:S(2)}, u32[]{:S(2)}) %collective-permute-start) | collective-permute-done | bytes 524320 | tf_op jit(solution)/shard_map/while/body/eval_jaxpr/ppermute | solution.py:16
  102.3 13.2 %collective-permute-done = f32[2,256,256]{2,1,0:T(8,128)S(1)} collective-permute-done((f32[2,256,256]{2,1,0:T(8,128)}, f32[2,256,256]{2,1,0:T(8,128)S(1)}, u32[]{:S(2)}, u32[]{:S(2)}) %collective-permute-start) | collective-permute-done | bytes 524320 | tf_op jit(solution)/shard_map/while/body/eval_jaxpr/ppermute | solution.py:16
  118.8 12.2 %collective-permute-done = f32[2,256,256]{2,1,0:T(8,128)S(1)} collective-permute-done((f32[2,256,256]{2,1,0:T(8,128)}, f32[2,256,256]{2,1,0:T(8,128)S(1)}, u32[]{:S(2)}, u32[]{:S(2)}) %collective-permute-start) | collective-permute-done | bytes 524320 | tf_op jit(solution)/shard_map/while/body/eval_jaxpr/ppermute | solution.py:16
  134.4 11.3 %collective-permute-done = f32[2,256,256]{2,1,0:T(8,128)S(1)} collective-permute-done((f32[2,256,256]{2,1,0:T(8,128)}, f32[2,256,256]{2,1,0:T(8,128)S(1)}, u32[]{:S(2)}, u32[]{:S(2)}) %collective-permute-start) | collective-permute-done | bytes 524320 | tf_op jit(solution)/shard_map/while/body/eval_jaxpr/ppermute | solution.py:16
  149.1 10.3 %collective-permute-done = f32[2,256,256]{2,1,0:T(8,128)S(1)} collective-permute-done((f32[2,256,256]{2,1,0:T(8,128)}, f32[2,256,256]{2,1,0:T(8,128)S(1)}, u32[]{:S(2)}, u32[]{:S(2)}) %collective-permute-start) | collective-permute-done | bytes 524320 | tf_op jit(solution)/shard_map/while/body/eval_jaxpr/ppermute | solution.py:16
  162.8 10.3 %collective-permute-done = f32[2,256,256]{2,1,0:T(8,128)S(1)} collective-permute-done((f32[2,256,256]{2,1,0:T(8,128)}, f32[2,256,256]{2,1,0:T(8,128)S(1)}, u32[]{:S(2)}, u32[]{:S(2)}) %collective-permute-start) | collective-permute-done | bytes 524320 | tf_op jit(solution)/shard_map/while/body/eval_jaxpr/ppermute | solution.py:16
  176.5 10.3 %collective-permute-done = f32[2,256,256]{2,1,0:T(8,128)S(1)} collective-permute-done((f32[2,256,256]{2,1,0:T(8,128)}, f32[2,256,256]{2,1,0:T(8,128)S(1)}, u32[]{:S(2)}, u32[]{:S(2)}) %collective-permute-start) | collective-permute-done | bytes 524320 | tf_op jit(solution)/shard_map/while/body/eval_jaxpr/ppermute | solution.py:16
  190.1 10.3 %collective-permute-done = f32[2,256,256]{2,1,0:T(8,128)S(1)} collective-permute-done((f32[2,256,256]{2,1,0:T(8,128)}, f32[2,256,256]{2,1,0:T(8,128)S(1)}, u32[]{:S(2)}, u32[]{:S(2)}) %collective-permute-start) | collective-permute-done | bytes 524320 | tf_op jit(solution)/shard_map/while/body/eval_jaxpr/ppermute | solution.py:16
  203.8 11.5 %collective-permute-done = f32[2,256,256]{2,1,0:T(8,128)S(1)} collective-permute-done((f32[2,256,256]{2,1,0:T(8,128)}, f32[2,256,256]{2,1,0:T(8,128)S(1)}, u32[]{:S(2)}, u32[]{:S(2)}) %collective-permute-start) | collective-permute-done | bytes 524320 | tf_op jit(solution)/shard_map/while/body/eval_jaxpr/ppermute | solution.py:16
  218.7 12.5 %collective-permute-done = f32[2,256,256]{2,1,0:T(8,128)S(1)} collective-permute-done((f32[2,256,256]{2,1,0:T(8,128)}, f32[2,256,256]{2,1,0:T(8,128)S(1)}, u32[]{:S(2)}, u32[]{:S(2)}) %collective-permute-start) | collective-permute-done | bytes 524320 | tf_op jit(solution)/shard_map/while/body/eval_jaxpr/ppermute | solution.py:16
  234.6 13.6 %collective-permute-done = f32[2,256,256]{2,1,0:T(8,128)S(1)} collective-permute-done((f32[2,256,256]{2,1,0:T(8,128)}, f32[2,256,256]{2,1,0:T(8,128)S(1)}, u32[]{:S(2)}, u32[]{:S(2)}) %collective-permute-start) | collective-permute-done | bytes 524320 | tf_op jit(solution)/shard_map/while/body/eval_jaxpr/ppermute | solution.py:16
  251.6 14.7 %collective-permute-done = f32[2,256,256]{2,1,0:T(8,128)S(1)} collective-permute-done((f32[2,256,256]{2,1,0:T(8,128)}, f32[2,256,256]{2,1,0:T(8,128)S(1)}, u32[]{:S(2)}, u32[]{:S(2)}) %collective-permute-start) | collective-permute-done | bytes 524320 | tf_op jit(solution)/shard_map/while/body/eval_jaxpr/ppermute | solution.py:16
  269.6 16.0 %collective-permute-done = f32[2,256,256]{2,1,0:T(8,128)S(1)} collective-permute-done((f32[2,256,256]{2,1,0:T(8,128)}, f32[2,256,256]{2,1,0:T(8,128)S(1)}, u32[]{:S(2)}, u32[]{:S(2)}) %collective-permute-start) | collective-permute-done | bytes 524320 | tf_op jit(solution)/shard_map/while/body/eval_jaxpr/ppermute | solution.py:16
  289.0 15.4 %collective-permute-done = f32[2,256,256]{2,1,0:T(8,128)S(1)} collective-permute-done((f32[2,256,256]{2,1,0:T(8,128)}, f32[2,256,256]{2,1,0:T(8,128)S(1)}, u32[]{:S(2)}, u32[]{:S(2)}) %collective-permute-start) | collective-permute-done | bytes 524320 | tf_op jit(solution)/shard_map/while/body/eval_jaxpr/ppermute | solution.py:16
  307.8 14.5 %collective-permute-done = f32[2,256,256]{2,1,0:T(8,128)S(1)} collective-permute-done((f32[2,256,256]{2,1,0:T(8,128)}, f32[2,256,256]{2,1,0:T(8,128)S(1)}, u32[]{:S(2)}, u32[]{:S(2)}) %collective-permute-start) | collective-permute-done | bytes 524320 | tf_op jit(solution)/shard_map/while/body/eval_jaxpr/ppermute | solution.py:16
  328.4 3.4 convert_bitcast_fusion.5
  343.3 3.2 copy-done.15
  356.3 3.3 copy-done.13
  359.6 7.2 %multiply_reduce_fusion.5 = (f32[]{:T(128)}, f32[2,16,256,256]{3,2,1,0:T(8,128)}) fusion(f32[]{:T(128)S(6)} %sqrt.12, f32[2,256,256]{2,1,0:T(8,128)S(1)} %get-tuple-element.67, bf16[1,2,16,256,256]{4,3,2,1,0:T(8,128)(2,1)S(1)} %copy-done, f32[2,16,256,256]{3,2,1,0:T(8,128)} %copy-done.13, f32[2]{0:T(128)S(1)} %get-tuple-element.44, ...), kind=kLoop, calls=%fused_computation.21 | loop fusion | flops 16777215 | bytes 29884440 | tf_op jit(solution)/shard_map/reduce_sum | solution.py:101
  366.8 29.8 %psum.50 = f32[]{:T(128)} all-reduce(f32[]{:T(128)} %get-tuple-element.57), channel_id=1, replica_groups=mesh['chain'=16,'sector'=8] {'sector'}, use_global_device_ids=true, to_apply=%region_5.6 | all-reduce | flops 1 | bytes 8 | tf_op jit(solution)/shard_map/psum | solution.py:101
  397.2 6.4 multiply_reduce_fusion.4
  403.6 13.1 %psum.51 = f32[]{:T(128)} all-reduce(f32[]{:T(128)} %multiply_reduce_fusion.4), channel_id=1, replica_groups=mesh['chain'=16,'sector'=8] {'sector'}, use_global_device_ids=true, to_apply=%region_7.8 | all-reduce | flops 1 | bytes 8 | tf_op jit(solution)/shard_map/psum | solution.py:103
  417.4 8.3 %subtract_divide_fusion.1 = f32[1,2,16,256,256]{4,3,2,1,0:T(8,128)S(1)} fusion(f32[1,2,16,256,256]{4,3,2,1,0:T(8,128)} %get-tuple-element.80, f32[1,2,16,256,256]{4,3,2,1,0:T(8,128)} %get-tuple-element.90, f32[]{:T(128)} %sqrt.13, f32[]{:T(128)} %div.85, f32[2]{0:T(128)S(1)} %get-tuple-element.44, f32[2]{0:T(128)S(1)} %get-tuple-element.43, f32[]{:T(128)S(6)} %sqrt.12, ...), kind=kLoop, calls=%fused_computation.20 | loop fusion | flops 18874368 | bytes 29884444 | tf_op jit(solution)/shard_map/div | solution.py:104
  425.7 11.9 %fusion.11 = bf16[2,256,256,16]{2,3,1,0:T(8,128)(2,1)} fusion(f32[2,16,256,256]{3,2,1,0:T(8,128)S(1)} %bitcast.419, f32[2,16,16]{2,1,0:T(8,128)S(1)} %broadcast_multiply_fusion.1), kind=kOutput, calls=%fused_computation.27 | convolution fusion | flops 402653184 | bytes 12591104 | tf_op jit(solution)/shard_map/pq,sqij->spij/dot_general | solution.py:44
  437.6 12.0 %fusion.13 = bf16[2,256,256,16]{2,3,1,0:T(8,128)(2,1)} fusion(f32[2,16,256,256]{3,2,1,0:T(8,128)S(1)} %bitcast.420, f32[2,16,16]{2,1,0:T(8,128)S(1)} %broadcast_multiply_fusion.1), kind=kOutput, calls=%fused_computation.29 | convolution fusion | flops 402653184 | bytes 12591104 | tf_op jit(solution)/shard_map/pq,sqij->spij/dot_general | solution.py:44
  449.5 7.5 %copy.82 = bf16[2,256,256,16]{1,2,3,0:T(8,128)(2,1)} copy(bf16[2,256,256,16]{2,3,1,0:T(8,128)(2,1)} %fusion.11) | data formatting | bytes 8388608 | tf_op jit(solution)/shard_map/pq,sqij->spij/dot_general | solution.py:44
  457.0 3.4 convert_bitcast_fusion.3
  465.4 3.4 bitcast_dynamic-update-slice_fusion.2
  471.3 7.7 %copy.75 = bf16[2,256,256,16]{1,2,3,0:T(8,128)(2,1)} copy(bf16[2,256,256,16]{2,3,1,0:T(8,128)(2,1)} %fusion.13) | data formatting | bytes 8388608 | tf_op jit(solution)/shard_map/pq,sqij->spij/dot_general | solution.py:44
  479.0 3.4 convert_bitcast_fusion.4
  490.4 3.2 copy-done.7
  498.7 3.2 copy-done.16
  502.8 8.1 %multiply_reduce_fusion.3 = f32[]{:T(128)} fusion(f32[2,16,256,256]{3,2,1,0:T(8,128)} %copy-done.7, f32[2]{0:T(128)S(1)} %get-tuple-element.44, f32[2,16,256,256]{3,2,1,0:T(8,128)} %bitcast_dynamic-update-slice_fusion.30, f32[2]{0:T(128)S(1)} %get-tuple-element.43, f32[]{:T(128)} %sqrt.13, f32[2,16,256,256]{3,2,1,0:T(8,128)S(1)} %bitcast.418, f32[]{:T(128)S(6)} %sqrt.12, ...), kind=kLoop, calls=%fused_computation.16 | loop fusion | flops 23068672 | bytes 29884448 | tf_op jit(solution)/shard_map/reduce_sum | solution.py:101
  510.9 13.1 %psum.52 = f32[]{:T(128)} all-reduce(f32[]{:T(128)} %multiply_reduce_fusion.3), channel_id=1, replica_groups=mesh['chain'=16,'sector'=8] {'sector'}, use_global_device_ids=true, to_apply=%region_9.10 | all-reduce | flops 1 | bytes 8 | tf_op jit(solution)/shard_map/psum | solution.py:101
  524.7 15.7 %multiply_reduce_fusion.2 = (f32[]{:T(128)}, f32[2,16,256,256]{3,2,1,0:T(8,128)}) fusion(f32[]{:T(128)} %sqrt.13, f32[2,16,256,256]{3,2,1,0:T(8,128)} %get-tuple-element.58, f32[]{:T(128)S(6)} %sqrt.12, f32[2,256,256]{2,1,0:T(8,128)S(1)} %get-tuple-element.67, bf16[1,2,16,256,256]{4,3,2,1,0:T(8,128)(2,1)} %param.11, f32[]{:T(128)} %div.85, f32[]{:T(128)} %div.92, ...), kind=kLoop, calls=%fused_computation.13 | loop fusion | flops 31457280 | bytes 38273060 | tf_op jit(solution)/shard_map/reduce_sum | solution.py:103
  540.4 13.3 %psum.53 = f32[]{:T(128)} all-reduce(f32[]{:T(128)} %get-tuple-element.55), channel_id=1, replica_groups=mesh['chain'=16,'sector'=8] {'sector'}, use_global_device_ids=true, to_apply=%region_11.12 | all-reduce | flops 1 | bytes 8 | tf_op jit(solution)/shard_map/psum | solution.py:103
  554.4 11.0 %subtract_divide_fusion = f32[1,2,16,256,256]{4,3,2,1,0:T(8,128)S(1)} fusion(f32[1,2,16,256,256]{4,3,2,1,0:T(8,128)} %copy-done.2, f32[1,2,16,256,256]{4,3,2,1,0:T(8,128)} %get-tuple-element.100, f32[1,2,16,256,256]{4,3,2,1,0:T(8,128)} %copy-done.16, f32[]{:T(128)} %sqrt.14, f32[]{:T(128)} %div.92, f32[]{:T(128)} %sqrt.13, f32[2]{0:T(128)S(1)} %get-tuple-element.44, ...), kind=kLoop, calls=%fused_computation.15 | loop fusion | flops 23068672 | bytes 38273056 | tf_op jit(solution)/shard_map/div | solution.py:104
  565.4 11.9 %fusion.7 = bf16[2,256,256,16]{2,3,1,0:T(8,128)(2,1)} fusion(f32[2,16,256,256]{3,2,1,0:T(8,128)S(1)} %bitcast.421, f32[2,16,16]{2,1,0:T(8,128)S(1)} %broadcast_multiply_fusion.1), kind=kOutput, calls=%fused_computation.23 | convolution fusion | flops 402653184 | bytes 12591104 | tf_op jit(solution)/shard_map/pq,sqij->spij/dot_general | solution.py:44
  577.3 12.3 %fusion.9 = bf16[2,256,256,16]{2,3,1,0:T(8,128)(2,1)} fusion(f32[2,16,256,256]{3,2,1,0:T(8,128)S(1)} %bitcast.422, f32[2,16,16]{2,1,0:T(8,128)S(1)} %broadcast_multiply_fusion.1), kind=kOutput, calls=%fused_computation.25 | convolution fusion | flops 402653184 | bytes 12591104 | tf_op jit(solution)/shard_map/pq,sqij->spij/dot_general | solution.py:44
  589.6 7.5 %copy.97 = bf16[2,256,256,16]{1,2,3,0:T(8,128)(2,1)} copy(bf16[2,256,256,16]{2,3,1,0:T(8,128)(2,1)} %fusion.7) | data formatting | bytes 8388608 | tf_op jit(solution)/shard_map/pq,sqij->spij/dot_general | solution.py:44
  597.1 3.4 convert_bitcast_fusion.1
  605.5 3.3 bitcast_dynamic-update-slice_fusion
  611.4 7.7 %copy.90 = bf16[2,256,256,16]{1,2,3,0:T(8,128)(2,1)} copy(bf16[2,256,256,16]{2,3,1,0:T(8,128)(2,1)} %fusion.9) | data formatting | bytes 8388608 | tf_op jit(solution)/shard_map/pq,sqij->spij/dot_general | solution.py:44
  619.0 3.4 convert_bitcast_fusion.2
  625.7 3.9 copy-done.14
  634.3 2.7 copy-done.6
  637.0 4.2 copy-done.5
  642.0 5.5 multiply_reduce_fusion.1
  647.5 13.1 %psum.54 = f32[]{:T(128)} all-reduce(f32[]{:T(128)} %multiply_reduce_fusion.1), channel_id=1, replica_groups=mesh['chain'=16,'sector'=8] {'sector'}, use_global_device_ids=true, to_apply=%region_13.14 | all-reduce | flops 1 | bytes 8 | tf_op jit(solution)/shard_map/psum | solution.py:101
  661.2 14.6 %multiply_reduce_fusion = f32[]{:T(128)} fusion(f32[]{:T(128)} %div.99, f32[]{:T(128)} %sqrt.14, f32[2,16,256,256]{3,2,1,0:T(8,128)} %get-tuple-element.56, f32[2,16,256,256]{3,2,1,0:T(8,128)} %copy-done.6, f32[2]{0:T(128)S(1)} %get-tuple-element.44, f32[2,16,256,256]{3,2,1,0:T(8,128)} %copy-done.5, f32[2]{0:T(128)S(1)} %get-tuple-element.43, f32[]{:T(128)} %sqrt.13, ...), kind=kLoop, calls=%fused_computation.10 | loop fusion | flops 33554432 | bytes 38273064 | tf_op jit(solution)/shard_map/reduce_sum | solution.py:103
  676.4 13.0 %psum.55 = f32[]{:T(128)} all-reduce(f32[]{:T(128)} %multiply_reduce_fusion), channel_id=1, replica_groups=mesh['chain'=16,'sector'=8] {'sector'}, use_global_device_ids=true, to_apply=%region_15.16 | all-reduce | flops 1 | bytes 8 | tf_op jit(solution)/shard_map/psum | solution.py:103
  690.7 20.4 %multiply_add_fusion = f32[1,2,16,256,256]{4,3,2,1,0:T(8,128)} fusion(f32[1,2,16,256,256]{4,3,2,1,0:T(8,128)} %copy-done.2, f32[1,2,16,256,256]{4,3,2,1,0:T(8,128)} %copy-done.3, f32[1,2,16,256,256]{4,3,2,1,0:T(8,128)} %get-tuple-element.120, f32[1,2,16,256,256]{4,3,2,1,0:T(8,128)} %get-tuple-element.130, f32[]{:T(128)} %sqrt.15, f32[]{:T(128)} %div.99, ...), kind=kLoop, calls=%fused_computation.9 | loop fusion | flops 37748736 | bytes 46661680 | tf_op jit(solution)/shard_map/add | solution.py:109
  (162 shorter events, 118.8 us)
Async XLA Ops:
  3.6 328.2 %collective-permute-start.2 = (bf16[2,2,256,256]{3,2,0,1:T(8,128)(2,1)S(1)}, bf16[2,2,256,256]{3,2,0,1:T(8,128)(2,1)}, u32[]{:S(2)}, u32[]{:S(2)}) collective-permute-start(bf16[2,2,256,256]{3,2,0,1:T(8,128)(2,1)S(1)} %bitcast_multiply_fusion), channel_id=1, source_target_pairs={{0,1},{1,2},{2,3},{3,4},{4,5},{5,6},{6,7},{8,9},{9,10},{10,11},{11... | collective-permute-start | bytes 1572872 | tf_op jit(solution)/shard_map/ppermute | solution.py:27
  7.3 326.6 %collective-permute-start.3 = (bf16[2,2,256,256]{3,2,0,1:T(8,128)(2,1)S(1)}, bf16[2,2,256,256]{3,2,0,1:T(8,128)(2,1)S(1)}, u32[]{:S(2)}, u32[]{:S(2)}) collective-permute-start(bf16[2,2,256,256]{3,2,0,1:T(8,128)(2,1)S(1)} %bitcast_multiply_fusion), channel_id=1, source_target_pairs={{1,0},{2,1},{3,2},{4,3},{5,4},{6,5},{7,6},{9,8},{10,9},{11,10},{12... | collective-permute-start | bytes 1572872 | tf_op jit(solution)/shard_map/ppermute | solution.py:29
  9.3 72.8 %collective-permute-start.1 = (f32[2,256,256]{2,1,0:T(8,128)S(1)}, f32[2,256,256]{2,1,0:T(8,128)S(1)}, u32[]{:S(2)}, u32[]{:S(2)}) collective-permute-start(f32[2,256,256]{2,1,0:T(8,128)S(1)} %get-tuple-element.66), channel_id=1, source_target_pairs={{0,8},{8,16},{16,24},{24,32},{32,40},{40,48},{48,56},{56,64},{64,7... | collective-permute-start | bytes 1572872 | tf_op jit(solution)/shard_map/ppermute | solution.py:16
  12.5 22.5 %copy-start.23 = (f32[2,16,16]{2,1,0:T(8,128)S(1)}, f32[2,16,16]{2,1,0:T(8,128)}, u32[]{:S(2)}) copy-start(f32[2,16,16]{2,1,0:T(8,128)} %param.15) | copy-start | bytes 6148
  12.5 22.5 %copy-start.24 = (f32[16,16]{1,0:T(8,128)S(1)}, f32[16,16]{1,0:T(8,128)}, u32[]{:S(2)}) copy-start(f32[16,16]{1,0:T(8,128)} %constant.27.clone) | copy-start | bytes 3076
  35.0 3.4 copy-start.4
  57.8 24.1 %copy-start.26 = (s32[2,2]{1,0:T(2,128)S(1)}, s32[2,2]{1,0:T(2,128)}, u32[]{:S(2)}) copy-start(s32[2,2]{1,0:T(2,128)} %param.16) | copy-start | bytes 52
  82.9 16.0 %collective-permute-start = (f32[2,256,256]{2,1,0:T(8,128)}, f32[2,256,256]{2,1,0:T(8,128)S(1)}, u32[]{:S(2)}, u32[]{:S(2)}) collective-permute-start(f32[2,256,256]{2,1,0:T(8,128)} %get-tuple-element.172), channel_id=1, source_target_pairs={{0,8},{8,16},{16,24},{24,32},{32,40},{40,48},{48,56},{56,64},{64,7... | collective-permute-start | bytes 1572872 | tf_op jit(solution)/shard_map/while/body/eval_jaxpr/ppermute | solution.py:16
  100.3 15.1 %collective-permute-start = (f32[2,256,256]{2,1,0:T(8,128)}, f32[2,256,256]{2,1,0:T(8,128)S(1)}, u32[]{:S(2)}, u32[]{:S(2)}) collective-permute-start(f32[2,256,256]{2,1,0:T(8,128)} %get-tuple-element.172), channel_id=1, source_target_pairs={{0,8},{8,16},{16,24},{24,32},{32,40},{40,48},{48,56},{56,64},{64,7... | collective-permute-start | bytes 1572872 | tf_op jit(solution)/shard_map/while/body/eval_jaxpr/ppermute | solution.py:16
  116.9 14.2 %collective-permute-start = (f32[2,256,256]{2,1,0:T(8,128)}, f32[2,256,256]{2,1,0:T(8,128)S(1)}, u32[]{:S(2)}, u32[]{:S(2)}) collective-permute-start(f32[2,256,256]{2,1,0:T(8,128)} %get-tuple-element.172), channel_id=1, source_target_pairs={{0,8},{8,16},{16,24},{24,32},{32,40},{40,48},{48,56},{56,64},{64,7... | collective-permute-start | bytes 1572872 | tf_op jit(solution)/shard_map/while/body/eval_jaxpr/ppermute | solution.py:16
  132.5 13.2 %collective-permute-start = (f32[2,256,256]{2,1,0:T(8,128)}, f32[2,256,256]{2,1,0:T(8,128)S(1)}, u32[]{:S(2)}, u32[]{:S(2)}) collective-permute-start(f32[2,256,256]{2,1,0:T(8,128)} %get-tuple-element.172), channel_id=1, source_target_pairs={{0,8},{8,16},{16,24},{24,32},{32,40},{40,48},{48,56},{56,64},{64,7... | collective-permute-start | bytes 1572872 | tf_op jit(solution)/shard_map/while/body/eval_jaxpr/ppermute | solution.py:16
  147.2 12.2 %collective-permute-start = (f32[2,256,256]{2,1,0:T(8,128)}, f32[2,256,256]{2,1,0:T(8,128)S(1)}, u32[]{:S(2)}, u32[]{:S(2)}) collective-permute-start(f32[2,256,256]{2,1,0:T(8,128)} %get-tuple-element.172), channel_id=1, source_target_pairs={{0,8},{8,16},{16,24},{24,32},{32,40},{40,48},{48,56},{56,64},{64,7... | collective-permute-start | bytes 1572872 | tf_op jit(solution)/shard_map/while/body/eval_jaxpr/ppermute | solution.py:16
  160.9 12.2 %collective-permute-start = (f32[2,256,256]{2,1,0:T(8,128)}, f32[2,256,256]{2,1,0:T(8,128)S(1)}, u32[]{:S(2)}, u32[]{:S(2)}) collective-permute-start(f32[2,256,256]{2,1,0:T(8,128)} %get-tuple-element.172), channel_id=1, source_target_pairs={{0,8},{8,16},{16,24},{24,32},{32,40},{40,48},{48,56},{56,64},{64,7... | collective-permute-start | bytes 1572872 | tf_op jit(solution)/shard_map/while/body/eval_jaxpr/ppermute | solution.py:16
  174.5 12.2 %collective-permute-start = (f32[2,256,256]{2,1,0:T(8,128)}, f32[2,256,256]{2,1,0:T(8,128)S(1)}, u32[]{:S(2)}, u32[]{:S(2)}) collective-permute-start(f32[2,256,256]{2,1,0:T(8,128)} %get-tuple-element.172), channel_id=1, source_target_pairs={{0,8},{8,16},{16,24},{24,32},{32,40},{40,48},{48,56},{56,64},{64,7... | collective-permute-start | bytes 1572872 | tf_op jit(solution)/shard_map/while/body/eval_jaxpr/ppermute | solution.py:16
  188.2 12.2 %collective-permute-start = (f32[2,256,256]{2,1,0:T(8,128)}, f32[2,256,256]{2,1,0:T(8,128)S(1)}, u32[]{:S(2)}, u32[]{:S(2)}) collective-permute-start(f32[2,256,256]{2,1,0:T(8,128)} %get-tuple-element.172), channel_id=1, source_target_pairs={{0,8},{8,16},{16,24},{24,32},{32,40},{40,48},{48,56},{56,64},{64,7... | collective-permute-start | bytes 1572872 | tf_op jit(solution)/shard_map/while/body/eval_jaxpr/ppermute | solution.py:16
  201.9 13.4 %collective-permute-start = (f32[2,256,256]{2,1,0:T(8,128)}, f32[2,256,256]{2,1,0:T(8,128)S(1)}, u32[]{:S(2)}, u32[]{:S(2)}) collective-permute-start(f32[2,256,256]{2,1,0:T(8,128)} %get-tuple-element.172), channel_id=1, source_target_pairs={{0,8},{8,16},{16,24},{24,32},{32,40},{40,48},{48,56},{56,64},{64,7... | collective-permute-start | bytes 1572872 | tf_op jit(solution)/shard_map/while/body/eval_jaxpr/ppermute | solution.py:16
  216.7 14.5 %collective-permute-start = (f32[2,256,256]{2,1,0:T(8,128)}, f32[2,256,256]{2,1,0:T(8,128)S(1)}, u32[]{:S(2)}, u32[]{:S(2)}) collective-permute-start(f32[2,256,256]{2,1,0:T(8,128)} %get-tuple-element.172), channel_id=1, source_target_pairs={{0,8},{8,16},{16,24},{24,32},{32,40},{40,48},{48,56},{56,64},{64,7... | collective-permute-start | bytes 1572872 | tf_op jit(solution)/shard_map/while/body/eval_jaxpr/ppermute | solution.py:16
  232.7 15.5 %collective-permute-start = (f32[2,256,256]{2,1,0:T(8,128)}, f32[2,256,256]{2,1,0:T(8,128)S(1)}, u32[]{:S(2)}, u32[]{:S(2)}) collective-permute-start(f32[2,256,256]{2,1,0:T(8,128)} %get-tuple-element.172), channel_id=1, source_target_pairs={{0,8},{8,16},{16,24},{24,32},{32,40},{40,48},{48,56},{56,64},{64,7... | collective-permute-start | bytes 1572872 | tf_op jit(solution)/shard_map/while/body/eval_jaxpr/ppermute | solution.py:16
  249.7 16.6 %collective-permute-start = (f32[2,256,256]{2,1,0:T(8,128)}, f32[2,256,256]{2,1,0:T(8,128)S(1)}, u32[]{:S(2)}, u32[]{:S(2)}) collective-permute-start(f32[2,256,256]{2,1,0:T(8,128)} %get-tuple-element.172), channel_id=1, source_target_pairs={{0,8},{8,16},{16,24},{24,32},{32,40},{40,48},{48,56},{56,64},{64,7... | collective-permute-start | bytes 1572872 | tf_op jit(solution)/shard_map/while/body/eval_jaxpr/ppermute | solution.py:16
  267.7 17.9 %collective-permute-start = (f32[2,256,256]{2,1,0:T(8,128)}, f32[2,256,256]{2,1,0:T(8,128)S(1)}, u32[]{:S(2)}, u32[]{:S(2)}) collective-permute-start(f32[2,256,256]{2,1,0:T(8,128)} %get-tuple-element.172), channel_id=1, source_target_pairs={{0,8},{8,16},{16,24},{24,32},{32,40},{40,48},{48,56},{56,64},{64,7... | collective-permute-start | bytes 1572872 | tf_op jit(solution)/shard_map/while/body/eval_jaxpr/ppermute | solution.py:16
  287.1 17.3 %collective-permute-start = (f32[2,256,256]{2,1,0:T(8,128)}, f32[2,256,256]{2,1,0:T(8,128)S(1)}, u32[]{:S(2)}, u32[]{:S(2)}) collective-permute-start(f32[2,256,256]{2,1,0:T(8,128)} %get-tuple-element.172), channel_id=1, source_target_pairs={{0,8},{8,16},{16,24},{24,32},{32,40},{40,48},{48,56},{56,64},{64,7... | collective-permute-start | bytes 1572872 | tf_op jit(solution)/shard_map/while/body/eval_jaxpr/ppermute | solution.py:16
  305.9 16.4 %collective-permute-start = (f32[2,256,256]{2,1,0:T(8,128)}, f32[2,256,256]{2,1,0:T(8,128)S(1)}, u32[]{:S(2)}, u32[]{:S(2)}) collective-permute-start(f32[2,256,256]{2,1,0:T(8,128)} %get-tuple-element.172), channel_id=1, source_target_pairs={{0,8},{8,16},{16,24},{24,32},{32,40},{40,48},{48,56},{56,64},{64,7... | collective-permute-start | bytes 1572872 | tf_op jit(solution)/shard_map/while/body/eval_jaxpr/ppermute | solution.py:16
  333.9 5.5 copy-start.10
  343.2 3.2 copy-start.15
  353.4 6.2 copy-start
  356.3 3.3 copy-start.13
  425.7 11.9 %copy-start.2 = (f32[1,2,16,256,256]{4,3,2,1,0:T(8,128)}, f32[1,2,16,256,256]{4,3,2,1,0:T(8,128)S(1)}, u32[]{:S(2)}) copy-start(f32[1,2,16,256,256]{4,3,2,1,0:T(8,128)S(1)} %subtract_divide_fusion.1) | copy-start | bytes 25165828
  460.5 8.3 %copy-start.9 = (bf16[2,16,256,256]{2,3,1,0:T(8,128)(2,1)}, bf16[2,16,256,256]{2,3,1,0:T(8,128)(2,1)S(1)}, u32[]{:S(2)}) copy-start(bf16[2,16,256,256]{2,3,1,0:T(8,128)(2,1)S(1)} %convert_bitcast_fusion.3) | copy-start | bytes 12582916
  484.2 1.4 copy-start.22
  484.2 2.2 copy-start.20
  484.2 2.9 copy-start.12
  485.0 2.9 copy-start.19
  488.1 14.6 %slice-start = ((s8[8388608]{0:T(1024)(128)(4,1)}), s8[4194304]{0:T(1024)(128)(4,1)S(1)}, s32[]{:S(2)}) async-start(s8[8388608]{0:T(1024)(128)(4,1)} %bitcast.417), calls=%async_computation | async-start | bytes 8388608
  490.4 3.2 copy-start.7
  493.6 9.1 %copy-start.1 = (bf16[1,2,16,256,256]{4,3,2,1,0:T(8,128)(2,1)S(1)}, bf16[1,2,16,256,256]{4,3,2,1,0:T(8,128)(2,1)}, u32[]{:S(2)}) copy-start(bf16[1,2,16,256,256]{4,3,2,1,0:T(8,128)(2,1)} %param.11) | copy-start | bytes 12582916
  495.1 7.7 %slice-start.1 = ((s8[8388608]{0:T(1024)(128)(4,1)}), s8[4194304]{0:T(1024)(128)(4,1)S(1)}, s32[]{:S(2)}) async-start(s8[8388608]{0:T(1024)(128)(4,1)} %bitcast.417), calls=%async_computation.1 | async-start | bytes 8388608
  498.7 3.2 copy-start.16
  565.4 11.9 %copy-start.3 = (f32[1,2,16,256,256]{4,3,2,1,0:T(8,128)}, f32[1,2,16,256,256]{4,3,2,1,0:T(8,128)S(1)}, u32[]{:S(2)}) copy-start(f32[1,2,16,256,256]{4,3,2,1,0:T(8,128)S(1)} %subtract_divide_fusion) | copy-start | bytes 25165828
  600.6 8.3 %copy-start.8 = (bf16[2,16,256,256]{2,3,1,0:T(8,128)(2,1)}, bf16[2,16,256,256]{2,3,1,0:T(8,128)(2,1)S(1)}, u32[]{:S(2)}) copy-start(bf16[2,16,256,256]{2,3,1,0:T(8,128)(2,1)S(1)} %convert_bitcast_fusion.1) | copy-start | bytes 12582916
  624.3 5.3 copy-start.21
  624.3 5.3 copy-start.17
  624.3 5.5 copy-start.11
  625.1 5.1 copy-start.18
  625.7 3.9 copy-start.14
  632.5 4.5 copy-start.6
  632.5 8.7 %slice-start.2 = ((s8[8388608]{0:T(1024)(128)(4,1)}), s8[4194304]{0:T(1024)(128)(4,1)S(1)}, s32[]{:S(2)}) async-start(s8[8388608]{0:T(1024)(128)(4,1)} %bitcast.423), calls=%async_computation.2 | async-start | bytes 8388608
  632.7 9.3 %slice-start.3 = ((s8[8388608]{0:T(1024)(128)(4,1)}), s8[4194304]{0:T(1024)(128)(4,1)S(1)}, s32[]{:S(2)}) async-start(s8[8388608]{0:T(1024)(128)(4,1)} %bitcast.423), calls=%async_computation.3 | async-start | bytes 8388608
  637.0 4.2 copy-start.5
  661.2 14.6 %copy-start.25 = (f32[1,4]{1,0:T(1,128)S(1)}, f32[1,4]{1,0:T(1,128)}, u32[]{:S(2)}) copy-start(f32[1,4]{1,0:T(1,128)} %param.18) | copy-start | bytes 52
where the time goes:
time: 720 us; the launch traced here: 711 us
  waiting for transfers between devices  189 us (26%)
  matrix products  170 us (24%)
  other arithmetic  110 us (15%)
  blocking collectives  109 us (15%)
  local copies, waits for them, and re-layouts  87.8 us (12%)
  starting transfers between devices  38.4 us (5%)
    ppermute x16, waiting for transfers between devices, from_behind(): return lax.ppermute(block, axis, route)  189 us
    dot_general x6, matrix products, apply_operator(): jnp.einsum('pq,sqij->spij', mixing[term], vector, precision=highest)  76.5 us
    psum x3, blocking collectives, on_device(): alpha = lax.psum(jnp.sum(current * image), 'sector') / count  55.9 us
    dot_general x30, matrix products, apply_operator(): jnp.einsum('spij,slj->spil', upper[:, begin:finish], picked, preferred_el...  48.9 us
    dot_general x6, local copies, waits for them, and re-layouts, apply_operator(): jnp.einsum('pq,sqij->spij', mixing[term], vector, precision=highest)  45.3 us
    unnamed x86, local copies, waits for them, and re-layouts  39.7 us
    psum x3, blocking collectives, on_device(): beta = jnp.sqrt(lax.psum(jnp.sum(image * image), 'sector') / count + eps)  39.4 us
    reduce_sum x3, other arithmetic, on_device(): beta = jnp.sqrt(lax.psum(jnp.sum(image * image), 'sector') / count + eps)  36.7 us
  transfers between devices with their start and end apart: 18, of which 15 were waited for; matrix products, arithmetic and copies ran while one was open for 12% of the time, Pallas kernels for 0%

commit v1 on v0

v1 whole, which is shorter than its diff:
```python
import functools

import jax
import jax.numpy as jnp
from jax import lax
from jax.experimental import pallas as pl
from jax.experimental.pallas import tpu as pltpu
from jax.sharding import PartitionSpec as P

f32, bf16 = jnp.float32, jnp.bfloat16
MESH = pl.DeviceIdType.MESH
group_bounds = [(0, 1), (1, 5), (5, 11), (11, 15), (15, 16)]
eps = 1e-6
LINE = 4
TOP = 32767.0


def split(x):
    high = x.astype(bf16)
    return high, (x - high.astype(f32)).astype(bf16)


def mm(a, b):
    return jnp.dot(a, b, preferred_element_type=f32)


def mm_nt(a, b):
    return lax.dot_general(a, b, (((1,), (1,)), ((), ())), preferred_element_type=f32)


def mm3(a, b):
    return mm(a[0], b[0]) + mm(a[0], b[1]) + mm(a[1], b[0])


def encode(x, ref):
    n = x.shape[0]
    top = jnp.max(jnp.abs(x), axis=0, keepdims=True)
    power = jnp.ceil(jnp.log2(jnp.maximum(top, 1e-35)) + 0.01)
    code = jnp.round(x * (jnp.exp2(-power) * TOP))
    ref[0:n] = code.astype(jnp.int32).astype(jnp.int16)
    ref[n : n + 16] = jnp.broadcast_to(power, (16, x.shape[1])).astype(jnp.int32).astype(jnp.int16)


def decode(ref):
    n = ref.shape[0] - 16
    power = ref[n : n + 16].astype(jnp.int32).astype(f32)[0:1]
    return ref[0:n].astype(jnp.int32).astype(f32) * (jnp.exp2(power) * (1.0 / TOP))


def fold(x):
    return jnp.sum(x.reshape(-1, 8, x.shape[-1]), axis=0)


def kernel(
    sizes, gates, ritz, theta, env_left, transfer, env_right, weights,
    u_out, w0_out, w1_out, w2_out, tri_out, coef_out,
    gbuf, tbuf, rbuf, wk, env, ypre, u, w0, w1, w2, mixed, half, ex_src, ex_dst,
    theta_sem, out_sem, g_send, g_recv, t_send, t_recv, r_send, r_recv, e_send, e_recv,
):
    nsec, nstate, n = u.shape[0], u.shape[1], u.shape[-1]
    chain, sector = lax.axis_index("chain"), lax.axis_index("sector")
    peers = ex_dst.shape[1]
    count = float(peers * nsec * nstate * n * n)
    z, y = chain // LINE, lax.rem(chain, LINE)

    theta_copy = pltpu.make_async_copy(theta.at[0], u, theta_sem)
    theta_copy.start()

    def on_y(d):
        return (z * LINE + lax.rem(y + d, LINE), sector)

    def on_z(d):
        return (lax.rem(z + d, LINE) * LINE + y, sector)

    def on_sector(d):
        return (chain, lax.rem(sector + d, peers))

    barrier = pltpu.get_barrier_semaphore()
    others = [on_y(1), on_y(LINE - 1), on_z(1), on_z(LINE - 1)] + [on_sector(d) for d in range(1, peers)]
    for other in others:
        pl.semaphore_signal(barrier, inc=1, device_id=other, device_id_type=MESH)

    rows = lax.broadcasted_iota(jnp.int32, (n, n), 0)
    cols = lax.broadcasted_iota(jnp.int32, (n, n), 1)

    def mask_of(s):
        return jnp.where((rows < sizes[s]) & (cols < sizes[s]), 1.0, 0.0).astype(f32)

    for s in range(nsec):
        mask = mask_of(s)
        encode(transfer[0, s] * mask, gbuf.at[0, s])
        for w in range(2):
            rbuf[2 + s, w] = (env_right[0, s, w].astype(f32) * mask).astype(bf16)
    pl.semaphore_wait(barrier, len(others))

    def remote(src, dst, send, recv, device):
        copy = pltpu.make_async_remote_copy(
            src_ref=src, dst_ref=dst, send_sem=send, recv_sem=recv,
            device_id=device, device_id_type=MESH,
        )
        copy.start()
        return copy

    def gather_start(buf, send, recv, onward, back):
        right0 = remote(buf.at[0, 0], buf.at[1, 0], send.at[0], recv.at[0], onward)
        left1 = remote(buf.at[0, 1], buf.at[3, 1], send.at[1], recv.at[1], back)
        right1 = remote(buf.at[0, 1], buf.at[1, 1], send.at[2], recv.at[2], onward)
        left0 = remote(buf.at[0, 0], buf.at[3, 0], send.at[3], recv.at[3], back)
        return right0, left1, right1, left0

    def gather_forward(copies, buf, send, recv, onward, back):
        copies[0].wait_recv()
        far0 = remote(buf.at[1, 0], buf.at[2, 0], send.at[4], recv.at[4], onward)
        copies[1].wait_recv()
        far1 = remote(buf.at[3, 1], buf.at[2, 1], send.at[5], recv.at[5], back)
        return copies + (far0, far1)

    def gather_finish(copies):
        for copy in copies[2:]:
            copy.wait_recv()
        for copy in copies:
            copy.wait_send()

    def exchange_start(e, sums):
        for i, x in enumerate(sums):
            ex_src[e, i] = x[:, :128] + x[:, 128:]
        for i in range(len(sums), ex_src.shape[1]):
            ex_src[e, i] = jnp.zeros((8, 128), f32)
        ex_dst[e, sector] = ex_src[e]
        return [
            remote(ex_src.at[e], ex_dst.at[e, sector], e_send.at[e, d], e_recv.at[e, d], on_sector(d))
            for d in range(1, peers)
        ]

    def exchange_finish(e, copies, amount):
        for copy in copies:
            copy.wait_recv()
        for copy in copies:
            copy.wait_send()
        total = ex_dst[e, 0]
        for d in range(1, peers):
            total = total + ex_dst[e, d]
        return [jnp.sum(jnp.sum(total[i], axis=0, keepdims=True), axis=1, keepdims=True) for i in range(amount)]

    def mix(src, s):
        def step(i, _):
            span = pl.ds(pl.multiple_of(i * 16, 16), 16)
            block = src[s, :, span, :].reshape(nstate * 16, n)
            out = mm(wk[...], block).astype(bf16).reshape(2, nstate, 16, n)
            mixed[s, :, :, span, :] = out
            return 0

        lax.fori_loop(0, n // 16, step, 0, unroll=True)

    def right_side(s):
        for level, (begin, finish) in enumerate(group_bounds):
            for w in range(2):
                def step(p, _):
                    half[s, p, w * n : (w + 1) * n, :] = mm_nt(mixed[s, w, p], rbuf[s + level, w]).astype(bf16)
                    return 0

                lax.fori_loop(begin, finish, step, 0, unroll=True)

    def both(f):
        def step(s, _):
            f(s)
            return 0

        lax.fori_loop(0, nsec, step, 0)

    def left_side(finish, sums):
        zero = tuple(jnp.zeros((8, n), f32) for _ in range(sums))

        def on_sec(s, accs):
            def on_state(p, accs):
                values = finish(s, p, mm(env[s], half[s, p]))
                return tuple(a + fold(v) for a, v in zip(accs, values))

            return lax.fori_loop(0, nstate, on_state, accs, unroll=True)

        return lax.fori_loop(0, nsec, on_sec, zero)

    ring_y = (on_y(1), on_y(LINE - 1))
    ring_z = (on_z(1), on_z(LINE - 1))
    copies = gather_start(gbuf, g_send, g_recv, *ring_y)
    halo = (
        remote(rbuf.at[pl.ds(2, 2)], rbuf.at[pl.ds(0, 2)], r_send.at[0], r_recv.at[0], on_sector(1)),
        remote(rbuf.at[pl.ds(2, 2)], rbuf.at[pl.ds(4, 2)], r_send.at[1], r_recv.at[1], on_sector(peers - 1)),
    )

    def charge(p):
        return sum((p >= bound).astype(jnp.int32) for bound in (1, 5, 11, 15))

    shape = (2 * nstate, nstate)
    state_row = lax.broadcasted_iota(jnp.int32, shape, 0) % nstate
    state_col = lax.broadcasted_iota(jnp.int32, shape, 1)
    table = jnp.where(charge(state_row) == charge(state_col), weights[...], 0.0).astype(bf16)
    tall = (2 * nstate * 16, 2 * nstate)
    spread_rows = jnp.where(
        lax.broadcasted_iota(jnp.int32, tall, 0) // 16 == lax.broadcasted_iota(jnp.int32, tall, 1), 1.0, 0.0
    ).astype(bf16)
    wide = (nstate, nstate * 16)
    spread_cols = jnp.where(
        lax.broadcasted_iota(jnp.int32, wide, 1) // 16 == lax.broadcasted_iota(jnp.int32, wide, 0), 1.0, 0.0
    ).astype(bf16)
    full = mm(mm(spread_rows, table).astype(bf16), spread_cols)
    big = full.shape
    same = lax.broadcasted_iota(jnp.int32, big, 0) % 16 == lax.broadcasted_iota(jnp.int32, big, 1) % 16
    wk[...] = jnp.where(same, full, 0.0).astype(bf16)

    theta_copy.wait()

    def masked(s, acc):
        mask = mask_of(s)

        def step(p, acc):
            value = u[s, p].astype(f32) * mask
            u[s, p] = value.astype(bf16)
            return acc + fold(value * value)

        return lax.fori_loop(0, nstate, step, acc, unroll=2)

    square = lax.fori_loop(0, nsec, masked, jnp.zeros((8, n), f32))
    started = exchange_start(0, [square])
    u_copy = pltpu.make_async_copy(u, u_out, out_sem.at[0])
    u_copy.start()
    mix(u, 0)
    copies = gather_forward(copies, gbuf, g_send, g_recv, *ring_y)
    mix(u, 1)
    gather_finish(copies)

    def slot(buf, at, j, s):
        return decode(buf.at[lax.rem(at - j + LINE, LINE), s])

    seconds = []
    for s in range(nsec):
        factors = [split(slot(gbuf, y, j, s)) for j in range(LINE)]
        second = mm3(factors[0], factors[1])
        later = mm3(factors[2], factors[3])
        ypre[s] = second
        encode(mm3(split(second), split(later)), tbuf.at[0, s])
    copies = gather_start(tbuf, t_send, t_recv, *ring_z)

    eye = jnp.where(rows == cols, 1.0, 0.0).astype(f32)

    def chosen(at, values):
        return jnp.where(
            at == 0, eye, jnp.where(at == 1, values[0], jnp.where(at == 2, values[1], values[2]))
        )

    for s in range(nsec):
        second = ypre[s]
        third = mm3(split(second), split(slot(gbuf, y, 2, s)))
        ypre[s] = chosen(y, (slot(gbuf, y, 0, s), second, third))
    for copy in halo:
        copy.wait()

    @pl.when(sector == 0)
    def _():
        rbuf[0:2] = jnp.zeros_like(rbuf[0:2])

    @pl.when(sector == peers - 1)
    def _():
        rbuf[4:6] = jnp.zeros_like(rbuf[4:6])

    (uu,) = exchange_finish(0, started, 1)
    right_side(0)
    copies = gather_forward(copies, tbuf, t_send, t_recv, *ring_z)
    right_side(1)
    gather_finish(copies)

    for s in range(nsec):
        first = slot(tbuf, z, 0, s)
        second = mm3(split(first), split(slot(tbuf, z, 1, s)))
        third = mm3(split(second), split(slot(tbuf, z, 2, s)))
        prefix = mm3(split(chosen(z, (first, second, third))), split(ypre[s]))
        high, low = split(prefix)
        high_t, low_t = split(prefix.T)
        mask = mask_of(s)
        for w in range(2):
            base = (env_left[s, w].astype(f32) * mask).astype(bf16)
            inner = split(mm(base, high) + mm(base, low))
            left = mm3((high_t, low_t), inner).astype(bf16).astype(f32) * gates[s, w].astype(f32)
            env[s, :, w * n : (w + 1) * n] = left.astype(bf16)

    def scalar(x):
        return x[0, 0]

    c0 = 1.0 / jnp.sqrt(uu / count + eps)
    c0_s = scalar(c0)

    def finish0(s, p, image):
        value = image * c0_s
        w0[s, p] = value.astype(bf16)
        return value * u[s, p].astype(f32), value * value

    started = exchange_start(1, left_side(finish0, 2))
    w0_copy = pltpu.make_async_copy(w0, w0_out, out_sem.at[1])
    w0_copy.start()
    both(lambda s: mix(w0, s))
    both(right_side)
    s1, s2 = exchange_finish(1, started, 2)

    def inverse(x):
        return 1.0 / x

    def root(x):
        return jnp.sqrt(jnp.maximum(x, 0.0) / count + eps)

    n00 = c0 * c0 * uu
    v0w0 = c0 * s1
    a0 = v0w0 / count
    r0 = s2 - 2.0 * a0 * v0w0 + a0 * a0 * n00
    b0 = root(r0)
    i0 = inverse(b0)
    n11 = r0 * i0 * i0
    n01 = (v0w0 - a0 * n00) * i0

    k_image, k_w0 = scalar(i0), scalar(a0 * i0)

    def finish1(s, p, image):
        before = w0[s, p].astype(f32)
        value = image * k_image - before * k_w0
        w1[s, p] = value.astype(bf16)
        return value * u[s, p].astype(f32), value * before, value * value

    started = exchange_start(2, left_side(finish1, 3))
    w1_copy = pltpu.make_async_copy(w1, w1_out, out_sem.at[2])
    w1_copy.start()
    both(lambda s: mix(w1, s))
    both(right_side)
    d0, d1, d2 = exchange_finish(2, started, 3)
    v0w1 = c0 * d0
    v1w1 = (d1 - a0 * v0w1) * i0
    a1 = v1w1 / count
    r1 = d2 + a1 * a1 * n11 + b0 * b0 * n00 - 2.0 * a1 * v1w1 - 2.0 * b0 * v0w1 + 2.0 * a1 * b0 * n01
    b1 = root(r1)
    i1 = inverse(b1)
    n22 = r1 * i1 * i1
    n12 = (v1w1 - a1 * n11 - b0 * n01) * i1

    k_image2, k_w1, k_w02 = scalar(i1), scalar(a1 * i1), scalar(b0 * i1)

    def finish2(s, p, image):
        older, before = w0[s, p].astype(f32), w1[s, p].astype(f32)
        value = image * k_image2 - before * k_w1 - older * k_w02
        w2[s, p] = value.astype(bf16)
        return value * u[s, p].astype(f32), value * older, value * before, value * value

    started = exchange_start(3, left_side(finish2, 4))
    w2_copy = pltpu.make_async_copy(w2, w2_out, out_sem.at[3])
    w2_copy.start()
    f0, f1, f2, f3 = exchange_finish(3, started, 4)
    v0w2 = c0 * f0
    v1w2 = (f1 - a0 * v0w2) * i0
    v2w2 = (f2 - a1 * v1w2 - b0 * v0w2) * i1
    a2 = v2w2 / count
    r2 = f3 + a2 * a2 * n22 + b1 * b1 * n11 - 2.0 * a2 * v2w2 - 2.0 * b1 * v1w2 + 2.0 * a2 * b1 * n12
    b2 = root(r2)
    k3 = ritz[0, 3] / b2
    m2 = ritz[0, 2] - k3 * a2
    m1 = ritz[0, 1] - k3 * b1 - m2 * a1 * i1
    m0 = ritz[0, 0] - m2 * b0 * i1 - m1 * a0 * i0
    for i, x in enumerate((a0, a1, a2, b0, b1, b2)):
        tri_out[i : i + 1, :] = jnp.broadcast_to(x, (1, 128))
    for i, x in enumerate((m0 * c0, m1 * i0, m2 * i1, k3)):
        coef_out[i : i + 1, :] = jnp.broadcast_to(x, (1, 128))
    for copy in (u_copy, w0_copy, w1_copy, w2_copy):
        copy.wait()


def combine(coef, u, w0, w1, w2, psi):
    total = u[...].astype(f32) * coef[0, 0]
    total = total + w0[...].astype(f32) * coef[1, 0]
    total = total + w1[...].astype(f32) * coef[2, 0]
    psi[...] = total + w2[...].astype(f32) * coef[3, 0]


def on_device(peers, theta, env_left0, transfer, env_right, mpo_weights, term_mask, block_sizes, ritz):
    _, nsec, nstate, n, _ = theta.shape
    field = jax.ShapeDtypeStruct((nsec, nstate, n, n), bf16)
    small = jax.ShapeDtypeStruct((8, 128), f32)
    smem = pl.BlockSpec(memory_space=pltpu.SMEM)
    vmem = pl.BlockSpec(memory_space=pltpu.VMEM)
    hbm = pl.BlockSpec(memory_space=pl.ANY)
    dma = pltpu.SemaphoreType.DMA
    code = pltpu.VMEM((4, nsec, n + 16, n), jnp.int16)
    stack = pltpu.VMEM((nsec, nstate, n, n), bf16)
    u, w0, w1, w2, tri, coef = pl.pallas_call(
        kernel,
        out_shape=(field, field, field, field, small, small),
        in_specs=[smem, smem, smem, hbm, vmem, vmem, vmem, vmem],
        out_specs=(hbm, hbm, hbm, hbm, vmem, vmem),
        scratch_shapes=[
            code, code,
            pltpu.VMEM((nsec + 4, 2, n, n), bf16),
            pltpu.VMEM((2 * nstate * 16, nstate * 16), bf16),
            pltpu.VMEM((nsec, n, 2 * n), bf16),
            pltpu.VMEM((nsec, n, n), f32),
            stack, stack, stack, stack,
            pltpu.VMEM((nsec, 2, nstate, n, n), bf16),
            pltpu.VMEM((nsec, nstate, 2 * n, n), bf16),
            pltpu.VMEM((4, 4, 8, 128), f32),
            pltpu.VMEM((4, peers, 4, 8, 128), f32),
            dma, dma((4,)), dma((6,)), dma((6,)), dma((6,)), dma((6,)),
            dma((2,)), dma((2,)), dma((4, peers)), dma((4, peers)),
        ],
        compiler_params=pltpu.CompilerParams(
            collective_id=0, has_side_effects=True, vmem_limit_bytes=56 * 2**20
        ),
    )(
        block_sizes, term_mask, ritz, theta, env_left0, transfer, env_right,
        mpo_weights.reshape(2 * nstate, nstate),
    )
    span = 1024
    total = nsec * nstate * n
    flat = [x.reshape(total, n) for x in (u, w0, w1, w2)]
    block = pl.BlockSpec((span, n), lambda i: (i, 0))
    psi = pl.pallas_call(
        combine,
        grid=(total // span,),
        out_shape=jax.ShapeDtypeStruct((total, n), f32),
        in_specs=[smem] + [block] * 4,
        out_specs=block,
        compiler_params=pltpu.CompilerParams(vmem_limit_bytes=24 * 2**20),
    )(coef, *flat)
    return psi.reshape(theta.shape), tri[:6, 0].reshape(1, 2, 3)


def solution(mesh):
    in_specs = (
        P("chain", "sector", None, None, None),
        P("sector", None, None, None),
        P("chain", "sector", None, None),
        P("chain", "sector", None, None, None),
        P(),
        P("sector", None),
        P("sector"),
        P("chain", None),
    )
    out_specs = (P("chain", "sector", None, None, None), P("chain", None, None))
    return jax.shard_map(
        functools.partial(on_device, mesh.shape["sector"]),
        mesh=mesh, in_specs=in_specs, out_specs=out_specs, check_vma=False,
    )
```

time: 720 us -> 81.4 us (0.11)
  the two profiles are of different devices: /device:TPU:97 before, /device:TPU:1 now
where the time goes in v1:
time: 81.4 us; the launch traced here: 81.1 us
  Pallas kernels  70.3 us (86%)
  local copies, waits for them, and re-layouts  10.2 us (13%)
    pallas_call x1, Pallas kernels, on_device(): pl.pallas_call(kernel, out_shape=(field, field, field, field, small, smal...  63.9 us
    unnamed x12, local copies, waits for them, and re-layouts  9.43 us
    pallas_call x1, Pallas kernels, on_device(): pl.pallas_call(combine, grid=(total // span,), out_shape=jax.ShapeDtypeSt...  6.41 us

profile of v1, /device:TPU:1, one launch (start us, length us, event | category | flops | bytes accessed | tf_op | source)
XLA Modules:
  0.0 81.1 jit_solution(14619370341401147665)
XLA Ops:
  0.6 63.9 %shard_map.95 = (bf16[2,16,256,256]{3,2,1,0:T(8,128)(2,1)}, bf16[2,16,256,256]{3,2,1,0:T(8,128)(2,1)}, bf16[2,16,256,256]{3,2,1,0:T(8,128)(2,1)}, bf16[2,16,256,...) custom-call(s32[2]{0:T(128)} %sizes.1, s32[2,2]{1,0:T(2,128)} %gates.1, f32[1,4]{1,0:T(1,128)} %ritz.1, ...), custom_call_target="tpu_custom_call" | custom-call | tf_op jit(solution)/shard_map/pallas_call | solution.py:389
  64.5 0.0 copy-start
  64.5 2.2 %copy-done = bf16[2,16,256,256]{3,2,1,0:T(8,128)(2,1)S(1)} copy-done((bf16[2,16,256,256]{3,2,1,0:T(8,128)(2,1)S(1)}, bf16[2,16,256,256]{3,2,1,0:T(8,128)(2,1)}, u32[]{:S(2)}) %copy-start) | copy-done | bytes 4194328
  66.7 0.0 copy-start.1
  66.7 2.2 %copy-done.1 = bf16[2,16,256,256]{3,2,1,0:T(8,128)(2,1)S(1)} copy-done((bf16[2,16,256,256]{3,2,1,0:T(8,128)(2,1)S(1)}, bf16[2,16,256,256]{3,2,1,0:T(8,128)(2,1)}, u32[]{:S(2)}) %copy-start.1) | copy-done | bytes 4194328
  68.9 0.0 copy-start.2
  68.9 2.2 %copy-done.2 = bf16[2,16,256,256]{3,2,1,0:T(8,128)(2,1)S(1)} copy-done((bf16[2,16,256,256]{3,2,1,0:T(8,128)(2,1)S(1)}, bf16[2,16,256,256]{3,2,1,0:T(8,128)(2,1)}, u32[]{:S(2)}) %copy-start.2) | copy-done | bytes 4194328
  71.1 0.0 copy-start.3
  71.1 2.2 %copy-done.3 = bf16[2,16,256,256]{3,2,1,0:T(8,128)(2,1)S(1)} copy-done((bf16[2,16,256,256]{3,2,1,0:T(8,128)(2,1)S(1)}, bf16[2,16,256,256]{3,2,1,0:T(8,128)(2,1)}, u32[]{:S(2)}) %copy-start.3) | copy-done | bytes 4194328
  73.3 0.0 copy-start.4
  73.3 0.7 copy-done.4
  73.9 0.0 copy-start.5
  73.9 6.4 %shard_map.96 = f32[8192,256]{1,0:T(8,128)} custom-call(f32[8,128]{1,0:T(8,128)S(1)} %copy-done.4, bf16[8192,256]{1,0:T(8,128)(2,1)S(1)} %bitcast.6, bf16[8192,256]{1,0:T(8,128)(2,1)S(1)} %bitcast.7, bf16[8192,256]{1,0:T(8,128)(2,1)S(1)} %bitcast.8, bf16[8192,256]{1,0:T(8,128)(2,1)S(1)} %bitcast.9), custom_call_target="tpu_custom_call" | custom-call | tf_op jit(solution)/shard_map/pallas_call | solution.py:419
  80.4 0.0 copy-done.5
  80.4 0.1 slice_reduce_fusion
  80.5 0.6 reshape_squeeze.3
Async XLA Ops:
  64.5 2.2 %copy-start = (bf16[2,16,256,256]{3,2,1,0:T(8,128)(2,1)S(1)}, bf16[2,16,256,256]{3,2,1,0:T(8,128)(2,1)}, u32[]{:S(2)}) copy-start(bf16[2,16,256,256]{3,2,1,0:T(8,128)(2,1)} %get-tuple-element.9) | copy-start | bytes 12582916
  66.7 2.2 %copy-start.1 = (bf16[2,16,256,256]{3,2,1,0:T(8,128)(2,1)S(1)}, bf16[2,16,256,256]{3,2,1,0:T(8,128)(2,1)}, u32[]{:S(2)}) copy-start(bf16[2,16,256,256]{3,2,1,0:T(8,128)(2,1)} %get-tuple-element.10) | copy-start | bytes 12582916
  68.9 2.2 %copy-start.2 = (bf16[2,16,256,256]{3,2,1,0:T(8,128)(2,1)S(1)}, bf16[2,16,256,256]{3,2,1,0:T(8,128)(2,1)}, u32[]{:S(2)}) copy-start(bf16[2,16,256,256]{3,2,1,0:T(8,128)(2,1)} %get-tuple-element.11) | copy-start | bytes 12582916
  71.1 2.2 %copy-start.3 = (bf16[2,16,256,256]{3,2,1,0:T(8,128)(2,1)S(1)}, bf16[2,16,256,256]{3,2,1,0:T(8,128)(2,1)}, u32[]{:S(2)}) copy-start(bf16[2,16,256,256]{3,2,1,0:T(8,128)(2,1)} %get-tuple-element.12) | copy-start | bytes 12582916
  73.3 0.7 copy-start.4
  73.9 6.4 %copy-start.5 = (f32[8,128]{1,0:T(8,128)S(1)}, f32[8,128]{1,0:T(8,128)}, u32[]{:S(2)}) copy-start(f32[8,128]{1,0:T(8,128)} %get-tuple-element.13) | copy-start | bytes 12292

commit v2 on v1

v2 whole, which is shorter than its diff:
```python
import functools

import jax
import jax.numpy as jnp
from jax import lax
from jax.experimental import pallas as pl
from jax.experimental.pallas import tpu as pltpu
from jax.sharding import PartitionSpec as P

f32, bf16 = jnp.float32, jnp.bfloat16
MESH = pl.DeviceIdType.MESH
group_bounds = [(0, 1), (1, 5), (5, 11), (11, 15), (15, 16)]
eps = 1e-6
LINE = 4
TOP = 32767.0


def split(x):
    high = x.astype(bf16)
    return high, (x - high.astype(f32)).astype(bf16)


def mm(a, b):
    return jnp.dot(a, b, preferred_element_type=f32)


def mm_nt(a, b):
    return lax.dot_general(a, b, (((1,), (1,)), ((), ())), preferred_element_type=f32)


def mm3(a, b):
    return mm(a[0], b[0]) + mm(a[0], b[1]) + mm(a[1], b[0])


def encode(x, ref):
    n = x.shape[0]
    top = jnp.max(jnp.abs(x), axis=0, keepdims=True)
    power = jnp.ceil(jnp.log2(jnp.maximum(top, 1e-35)) + 0.01)
    code = jnp.round(x * (jnp.exp2(-power) * TOP))
    ref[0:n] = code.astype(jnp.int32).astype(jnp.int16)
    ref[n : n + 16] = jnp.broadcast_to(power, (16, x.shape[1])).astype(jnp.int32).astype(jnp.int16)


def decode(ref):
    n = ref.shape[0] - 16
    power = ref[n : n + 16].astype(jnp.int32).astype(f32)[0:1]
    return ref[0:n].astype(jnp.int32).astype(f32) * (jnp.exp2(power) * (1.0 / TOP))


def fold(x):
    return jnp.sum(x.reshape(-1, 8, x.shape[-1]), axis=0)


def kernel(
    sizes, gates, ritz, theta, env_left, transfer, env_right, weights,
    u, w0, w1, w2, tri_out, coef_out,
    gbuf, tbuf, rbuf, wk, env, ypre, mixed, half, ex_src, ex_dst, factor, base_env,
    in_sem, g_send, g_recv, t_send, t_recv, r_send, r_recv, e_send, e_recv,
):
    nsec, nstate, n = u.shape[0], u.shape[1], u.shape[-1]
    chain, sector = lax.axis_index("chain"), lax.axis_index("sector")
    peers = ex_dst.shape[1]
    count = float(peers * nsec * nstate * n * n)
    z, y = chain // LINE, lax.rem(chain, LINE)

    def on_y(d):
        return (z * LINE + lax.rem(y + d, LINE), sector)

    def on_z(d):
        return (lax.rem(z + d, LINE) * LINE + y, sector)

    def on_sector(d):
        return (chain, lax.rem(sector + d, peers))

    barrier = pltpu.get_barrier_semaphore()
    others = [on_y(1), on_y(LINE - 1), on_z(1), on_z(LINE - 1)] + [on_sector(d) for d in range(1, peers)]
    for other in others:
        pl.semaphore_signal(barrier, inc=1, device_id=other, device_id_type=MESH)

    incoming = [
        pltpu.make_async_copy(src, dst, in_sem.at[i])
        for i, (src, dst) in enumerate((
            (transfer.at[0], factor), (env_right.at[0], rbuf.at[pl.ds(2, 2)]), (theta.at[0], u), (env_left, base_env),
        ))
    ]
    for copy in incoming:
        copy.start()
    rows = lax.broadcasted_iota(jnp.int32, (n, n), 0)
    cols = lax.broadcasted_iota(jnp.int32, (n, n), 1)

    def mask_of(s):
        return jnp.where((rows < sizes[s]) & (cols < sizes[s]), 1.0, 0.0).astype(f32)

    incoming[0].wait()
    for s in range(nsec):
        encode(factor[s] * mask_of(s), gbuf.at[0, s])
    pl.semaphore_wait(barrier, len(others))

    def remote(src, dst, send, recv, device):
        copy = pltpu.make_async_remote_copy(
            src_ref=src, dst_ref=dst, send_sem=send, recv_sem=recv,
            device_id=device, device_id_type=MESH,
        )
        copy.start()
        return copy

    pending = []
    upper, lower = pl.ds(0, n // 2), pl.ds(n // 2, n // 2 + 16)

    def line_send(buf, s, send, recv, onward, back):
        plan = ((1, upper, onward), (3, lower, back), (1, lower, onward), (3, upper, back))
        copies = [
            remote(buf.at[0, s, part], buf.at[place, s, part], send.at[s, i], recv.at[s, i], device)
            for i, (place, part, device) in enumerate(plan)
        ]
        pending.extend(copies)
        return copies

    def line_forward(copies, buf, s, send, recv, onward, back):
        for i, (place, part, device) in enumerate(((1, upper, onward), (3, lower, back))):
            copies[i].wait_recv()
            copy = remote(buf.at[place, s, part], buf.at[2, s, part], send.at[s, 4 + i], recv.at[s, 4 + i], device)
            copies.append(copy)
            pending.append(copy)

    def line_finish(copies):
        for copy in copies[2:]:
            copy.wait_recv()

    def exchange_start(e, sums):
        for i, x in enumerate(sums):
            ex_src[e, i] = x[:, :128] + x[:, 128:]
        for i in range(len(sums), ex_src.shape[1]):
            ex_src[e, i] = jnp.zeros((8, 128), f32)
        ex_dst[e, sector] = ex_src[e]
        copies = [
            remote(ex_src.at[e], ex_dst.at[e, sector], e_send.at[e, d], e_recv.at[e, d], on_sector(d))
            for d in range(1, peers)
        ]
        pending.extend(copies)
        return copies

    def exchange_finish(e, copies, amount):
        for copy in copies:
            copy.wait_recv()
        total = ex_dst[e, 0]
        for d in range(1, peers):
            total = total + ex_dst[e, d]
        return [jnp.sum(jnp.sum(total[i], axis=0, keepdims=True), axis=1, keepdims=True) for i in range(amount)]

    def mix(src, s):
        def step(i, _):
            span = pl.ds(pl.multiple_of(i * 16, 16), 16)
            block = src[s, :, span, :].reshape(nstate * 16, n)
            out = mm(wk[...], block).astype(bf16).reshape(2, nstate, 16, n)
            mixed[s, :, :, span, :] = out
            return 0

        lax.fori_loop(0, n // 16, step, 0, unroll=True)

    def right_side(s):
        for level, (begin, finish) in enumerate(group_bounds):
            for w in range(2):
                def step(p, _):
                    half[s, p, w * n : (w + 1) * n, :] = mm_nt(mixed[s, w, p], rbuf[s + level, w]).astype(bf16)
                    return 0

                lax.fori_loop(begin, finish, step, 0, unroll=True)

    def left_of(finish, s, accs):
        def on_state(p, accs):
            values = finish(s, p, mm(env[s], half[s, p]))
            return tuple(a + fold(v) for a, v in zip(accs, values))

        return lax.fori_loop(0, nstate, on_state, accs, unroll=True)

    def zeros(sums):
        return tuple(jnp.zeros((8, n), f32) for _ in range(sums))

    def left_side(finish, sums):
        return lax.fori_loop(0, nsec, lambda s, accs: left_of(finish, s, accs), zeros(sums))

    ring_y = (g_send, g_recv, on_y(1), on_y(LINE - 1))
    ring_z = (t_send, t_recv, on_z(1), on_z(LINE - 1))
    copies = [line_send(gbuf, s, *ring_y) for s in range(nsec)]
    incoming[1].wait()
    for s in range(nsec):
        mask = mask_of(s)
        for w in range(2):
            rbuf[2 + s, w] = (rbuf[2 + s, w].astype(f32) * mask).astype(bf16)
    halo = (
        remote(rbuf.at[pl.ds(2, 2)], rbuf.at[pl.ds(0, 2)], r_send.at[0], r_recv.at[0], on_sector(1)),
        remote(rbuf.at[pl.ds(2, 2)], rbuf.at[pl.ds(4, 2)], r_send.at[1], r_recv.at[1], on_sector(peers - 1)),
    )

    def charge(p):
        return sum((p >= bound).astype(jnp.int32) for bound in (1, 5, 11, 15))

    shape = (2 * nstate, nstate)
    state_row = lax.broadcasted_iota(jnp.int32, shape, 0) % nstate
    state_col = lax.broadcasted_iota(jnp.int32, shape, 1)
    table = jnp.where(charge(state_row) == charge(state_col), weights[...], 0.0).astype(bf16)
    tall = (2 * nstate * 16, 2 * nstate)
    spread_rows = jnp.where(
        lax.broadcasted_iota(jnp.int32, tall, 0) // 16 == lax.broadcasted_iota(jnp.int32, tall, 1), 1.0, 0.0
    ).astype(bf16)
    wide = (nstate, nstate * 16)
    spread_cols = jnp.where(
        lax.broadcasted_iota(jnp.int32, wide, 1) // 16 == lax.broadcasted_iota(jnp.int32, wide, 0), 1.0, 0.0
    ).astype(bf16)
    full = mm(mm(spread_rows, table).astype(bf16), spread_cols)
    big = full.shape
    same = lax.broadcasted_iota(jnp.int32, big, 0) % 16 == lax.broadcasted_iota(jnp.int32, big, 1) % 16
    wk[...] = jnp.where(same, full, 0.0).astype(bf16)

    incoming[2].wait()

    def masked(s, acc):
        mask = mask_of(s)

        def step(p, acc):
            value = u[s, p].astype(f32) * mask
            u[s, p] = value.astype(bf16)
            return acc + fold(value * value)

        return lax.fori_loop(0, nstate, step, acc, unroll=2)

    square = lax.fori_loop(0, nsec, masked, jnp.zeros((8, n), f32))
    started = exchange_start(0, [square])
    for s in range(nsec):
        line_forward(copies[s], gbuf, s, *ring_y)
        mix(u, s)

    def slot(buf, at, j, s):
        return decode(buf.at[lax.rem(at - j + LINE, LINE), s])

    for s in range(nsec):
        line_finish(copies[s])
        factors = [split(slot(gbuf, y, j, s)) for j in range(LINE)]
        second = mm3(factors[0], factors[1])
        later = mm3(factors[2], factors[3])
        ypre[s] = second
        encode(mm3(split(second), split(later)), tbuf.at[0, s])
        copies[s] = line_send(tbuf, s, *ring_z)

    eye = jnp.where(rows == cols, 1.0, 0.0).astype(f32)

    def chosen(at, values):
        return jnp.where(
            at == 0, eye, jnp.where(at == 1, values[0], jnp.where(at == 2, values[1], values[2]))
        )

    for s in range(nsec):
        second = ypre[s]
        third = mm3(split(second), split(slot(gbuf, y, 2, s)))
        ypre[s] = chosen(y, (slot(gbuf, y, 0, s), second, third))
    for copy in halo:
        copy.wait_recv()
    pending.extend(halo)

    @pl.when(sector == 0)
    def _():
        rbuf[0:2] = jnp.zeros_like(rbuf[0:2])

    @pl.when(sector == peers - 1)
    def _():
        rbuf[4:6] = jnp.zeros_like(rbuf[4:6])

    incoming[3].wait()
    (uu,) = exchange_finish(0, started, 1)
    for s in range(nsec):
        right_side(s)
        line_forward(copies[s], tbuf, s, *ring_z)

    inv_count = 1.0 / count

    def row(x):
        return jnp.broadcast_to(x, (1, n))

    c0 = 1.0 / jnp.sqrt(uu * inv_count + eps)
    k_c0 = row(c0)

    def finish0(s, p, image):
        value = image * k_c0
        w0[s, p] = value.astype(bf16)
        return value * u[s, p].astype(f32), value * value

    sums = zeros(2)
    for s in range(nsec):
        line_finish(copies[s])
        near = [jnp.where(z > j, slot(tbuf, z, j, s), eye) for j in range(LINE - 1)]
        front = mm3(split(near[0]), split(near[1]))
        back = mm3(split(near[2]), split(ypre[s]))
        prefix = mm3(split(front), split(back))
        high, low = split(prefix)
        high_t, low_t = split(prefix.T)
        mask = mask_of(s)
        for w in range(2):
            base = (base_env[s, w].astype(f32) * mask).astype(bf16)
            inner = split(mm(base, high) + mm(base, low))
            left = mm3((high_t, low_t), inner).astype(bf16).astype(f32) * gates[s, w].astype(f32)
            env[s, :, w * n : (w + 1) * n] = left.astype(bf16)
        sums = left_of(finish0, s, sums)
    started = exchange_start(1, sums)
    mix(w0, 0)
    right_side(0)
    mix(w0, 1)
    s1, s2 = exchange_finish(1, started, 2)

    def inverse(x):
        return 1.0 / x

    def root(x):
        return jnp.sqrt(jnp.maximum(x, 0.0) * inv_count + eps)

    n00 = c0 * c0 * uu
    v0w0 = c0 * s1
    a0 = v0w0 * inv_count
    r0 = s2 - 2.0 * a0 * v0w0 + a0 * a0 * n00
    b0 = root(r0)
    i0 = inverse(b0)
    n11 = r0 * i0 * i0
    n01 = (v0w0 - a0 * n00) * i0

    k_image, k_w0 = row(i0), row(a0 * i0)
    right_side(1)

    def finish1(s, p, image):
        before = w0[s, p].astype(f32)
        value = image * k_image - before * k_w0
        w1[s, p] = value.astype(bf16)
        return value * u[s, p].astype(f32), value * before, value * value

    started = exchange_start(2, left_side(finish1, 3))
    mix(w1, 0)
    right_side(0)
    mix(w1, 1)
    d0, d1, d2 = exchange_finish(2, started, 3)
    v0w1 = c0 * d0
    v1w1 = (d1 - a0 * v0w1) * i0
    a1 = v1w1 * inv_count
    r1 = d2 + a1 * a1 * n11 + b0 * b0 * n00 - 2.0 * a1 * v1w1 - 2.0 * b0 * v0w1 + 2.0 * a1 * b0 * n01
    b1 = root(r1)
    i1 = inverse(b1)
    n22 = r1 * i1 * i1
    n12 = (v1w1 - a1 * n11 - b0 * n01) * i1

    k_image2, k_w1, k_w02 = row(i1), row(a1 * i1), row(b0 * i1)
    right_side(1)

    def finish2(s, p, image):
        older, before = w0[s, p].astype(f32), w1[s, p].astype(f32)
        value = image * k_image2 - before * k_w1 - older * k_w02
        w2[s, p] = value.astype(bf16)
        return value * u[s, p].astype(f32), value * older, value * before, value * value

    started = exchange_start(3, left_side(finish2, 4))
    f0, f1, f2, f3 = exchange_finish(3, started, 4)
    v0w2 = c0 * f0
    v1w2 = (f1 - a0 * v0w2) * i0
    v2w2 = (f2 - a1 * v1w2 - b0 * v0w2) * i1
    a2 = v2w2 * inv_count
    r2 = f3 + a2 * a2 * n22 + b1 * b1 * n11 - 2.0 * a2 * v2w2 - 2.0 * b1 * v1w2 + 2.0 * a2 * b1 * n12
    b2 = root(r2)
    k3 = ritz[0, 3] / b2
    m2 = ritz[0, 2] - k3 * a2
    m1 = ritz[0, 1] - k3 * b1 - m2 * a1 * i1
    m0 = ritz[0, 0] - m2 * b0 * i1 - m1 * a0 * i0
    lane = lax.broadcasted_iota(jnp.int32, (1, 128), 1)
    for i, (x, y0, y1) in enumerate(((a0, a1, a2), (b0, b1, b2))):
        tri_out[i : i + 1, :] = jnp.where(lane == 0, x, jnp.where(lane == 1, y0, y1))
    for i, x in enumerate((m0 * c0, m1 * i0, m2 * i1, k3)):
        coef_out[i : i + 1, :] = row(x)
    for copy in pending:
        copy.wait_send()


def combine(coef, tri, u, w0, w1, w2, psi, tri_out, block, sems):
    tri_out[0] = tri[0:2, 0:3]
    parts = sems.shape[0]
    span = u.shape[0] // parts
    weights = [coef[i : i + 1, :] for i in range(4)]
    copies = []
    for part in range(parts):
        rows = pl.ds(part * span, span)

        def step(i, _):
            some = pl.ds(pl.multiple_of(part * span + i * 64, 64), 64)
            total = u[some, :].astype(f32) * weights[0]
            total = total + w0[some, :].astype(f32) * weights[1]
            total = total + w1[some, :].astype(f32) * weights[2]
            block[some, :] = total + w2[some, :].astype(f32) * weights[3]
            return 0

        lax.fori_loop(0, span // 64, step, 0, unroll=4)
        copy = pltpu.make_async_copy(block.at[rows], psi.at[rows], sems.at[part])
        copy.start()
        copies.append(copy)
    for copy in copies:
        copy.wait()


def on_device(peers, theta, env_left0, transfer, env_right, mpo_weights, term_mask, block_sizes, ritz):
    _, nsec, nstate, n, _ = theta.shape
    field = pltpu.VMEM((nsec, nstate, n, n), bf16)
    smem = pl.BlockSpec(memory_space=pltpu.SMEM)
    vmem = pl.BlockSpec(memory_space=pltpu.VMEM)
    hbm = pl.BlockSpec(memory_space=pl.ANY)
    dma = pltpu.SemaphoreType.DMA
    code = pltpu.VMEM((4, nsec, n + 16, n), jnp.int16)
    u, w0, w1, w2, tri, coef = pl.pallas_call(
        kernel,
        out_shape=(field, field, field, field, pltpu.VMEM((8, 128), f32), pltpu.VMEM((8, n), f32)),
        in_specs=[smem, smem, smem, hbm, hbm, hbm, hbm, vmem],
        out_specs=(vmem,) * 6,
        scratch_shapes=[
            code, code,
            pltpu.VMEM((nsec + 4, 2, n, n), bf16),
            pltpu.VMEM((2 * nstate * 16, nstate * 16), bf16),
            pltpu.VMEM((nsec, n, 2 * n), bf16),
            pltpu.VMEM((nsec, n, n), f32),
            pltpu.VMEM((nsec, 2, nstate, n, n), bf16),
            pltpu.VMEM((nsec, nstate, 2 * n, n), bf16),
            pltpu.VMEM((4, 4, 8, 128), f32),
            pltpu.VMEM((4, peers, 4, 8, 128), f32),
            pltpu.VMEM((nsec, n, n), f32),
            pltpu.VMEM((nsec, 2, n, n), bf16),
            dma((4,)), dma((nsec, 6)), dma((nsec, 6)), dma((nsec, 6)), dma((nsec, 6)),
            dma((2,)), dma((2,)), dma((4, peers)), dma((4, peers)),
        ],
        compiler_params=pltpu.CompilerParams(
            collective_id=0, has_side_effects=True, vmem_limit_bytes=40 * 2**20
        ),
    )(
        block_sizes, term_mask, ritz, theta, env_left0, transfer, env_right,
        mpo_weights.reshape(2 * nstate, nstate),
    )
    total = nsec * nstate * n
    flat = [x.reshape(total, n) for x in (u, w0, w1, w2)]
    parts = 16
    psi, tridiag = pl.pallas_call(
        combine,
        out_shape=(jax.ShapeDtypeStruct((total, n), f32), jax.ShapeDtypeStruct((1, 2, 3), f32)),
        in_specs=[vmem] * 6,
        out_specs=(hbm, vmem),
        scratch_shapes=[pltpu.VMEM((total, n), f32), dma((parts,))],
        compiler_params=pltpu.CompilerParams(vmem_limit_bytes=24 * 2**20),
    )(coef, tri, *flat)
    return psi.reshape(theta.shape), tridiag


def solution(mesh):
    in_specs = (
        P("chain", "sector", None, None, None),
        P("sector", None, None, None),
        P("chain", "sector", None, None),
        P("chain", "sector", None, None, None),
        P(),
        P("sector", None),
        P("sector"),
        P("chain", None),
    )
    out_specs = (P("chain", "sector", None, None, None), P("chain", None, None))
    return jax.shard_map(
        functools.partial(on_device, mesh.shape["sector"]),
        mesh=mesh, in_specs=in_specs, out_specs=out_specs, check_vma=False,
    )
```

time: 81.4 us -> 66.2 us (0.81)
  local copies, waits for them, and re-layouts: 10.2 us -> 0 us
  Pallas kernels: 70.3 us -> 65.2 us
    unnamed x12 -> x0, local copies, waits for them, and re-layouts: 9.43 us -> none
    pallas_call x2, Pallas kernels: 70.3 us -> 65.2 us  [the longest x1 60.2 us: on_device(): pl.pallas_call(kernel, out_shape=(field, field, field, field, pltpu.VMEM(...]
where the time goes in v2:
time: 66.2 us; the launch traced here: 66.1 us
  Pallas kernels  65.2 us (98%)
  between operations  0.82 us (1%)
    pallas_call x1, Pallas kernels, on_device(): pl.pallas_call(kernel, out_shape=(field, field, field, field, pltpu.VMEM(...  60.2 us
    pallas_call x1, Pallas kernels, on_device(): pl.pallas_call(combine, out_shape=(jax.ShapeDtypeStruct((total, n), f32),...  5.03 us

profile of v2, /device:TPU:1, one launch (start us, length us, event | category | flops | bytes accessed | tf_op | source)
XLA Modules:
  0.0 66.1 jit_solution(3291577029486637083)
XLA Ops:
  0.6 60.2 %shard_map.95 = (bf16[2,16,256,256]{3,2,1,0:T(8,128)(2,1)S(1)}, bf16[2,16,256,256]{3,2,1,0:T(8,128)(2,1)S(1)}, bf16[2,16,256,256]{3,2,1,0:T(8,128)(2,1)S(1)}, bf...) custom-call(s32[2]{0:T(128)} %sizes.1, s32[2,2]{1,0:T(2,128)} %gates.1, ...), custom_call_target="tpu_custom_call" | custom-call | tf_op jit(solution)/shard_map/pallas_call | solution.py:411
  60.9 5.0 %shard_map.96 = (f32[8192,256]{1,0:T(8,128)}, f32[1,2,3]{2,1,0:T(2,128)}) custom-call(f32[8,256]{1,0:T(8,128)S(1)} %get-tuple-element.10.coef, f32[8,128]{1,0:T(8,128)S(1)} %get-tuple-element.11.tri, bf16[8192,256]{1,0:T(8,128)(2,1)S(1)} %bitcast.6, bf16[8192,256]{1,0:T(8,128)(2,1)S(1)} %bitcast.7, bf16[8192,256]{1,0:T(8,128)(2,1)S(1)} %bitcast.8, ...), custom_call_target="tpu_custom_call" | custom-call | tf_op jit(solution)/shard_map/pallas_call | solution.py:441

commit v3 on v2

--- a/solution.py
+++ b/solution.py
@@ -128,15 +128,16 @@
             copy.wait_recv()
 
     def exchange_start(e, sums):
+        place = lax.broadcasted_iota(jnp.int32, (8, 128), 0)
+        tile = jnp.zeros((8, 128), f32)
         for i, x in enumerate(sums):
-            ex_src[e, i] = x[:, :128] + x[:, 128:]
-        for i in range(len(sums), ex_src.shape[1]):
-            ex_src[e, i] = jnp.zeros((8, 128), f32)
-        ex_dst[e, sector] = ex_src[e]
+            tile = jnp.where(place == i, jnp.sum(x[:, :128] + x[:, 128:], axis=0, keepdims=True), tile)
+        ex_src[e] = tile
         copies = [
             remote(ex_src.at[e], ex_dst.at[e, sector], e_send.at[e, d], e_recv.at[e, d], on_sector(d))
             for d in range(1, peers)
         ]
+        ex_dst[e, sector] = tile
         pending.extend(copies)
         return copies
 
@@ -146,7 +147,8 @@
         total = ex_dst[e, 0]
         for d in range(1, peers):
             total = total + ex_dst[e, d]
-        return [jnp.sum(jnp.sum(total[i], axis=0, keepdims=True), axis=1, keepdims=True) for i in range(amount)]
+        sums = jnp.sum(total, axis=1, keepdims=True)
+        return [sums[i : i + 1] for i in range(amount)]
 
     def mix(src, s):
         def step(i, _):
@@ -158,8 +160,9 @@
 
         lax.fori_loop(0, n // 16, step, 0, unroll=True)
 
-    def right_side(s):
-        for level, (begin, finish) in enumerate(group_bounds):
+    def right_side(s, levels=range(5)):
+        for level in levels:
+            begin, finish = group_bounds[level]
             for w in range(2):
                 def step(p, _):
                     half[s, p, w * n : (w + 1) * n, :] = mm_nt(mixed[s, w, p], rbuf[s + level, w]).astype(bf16)
@@ -305,6 +308,7 @@
     mix(w0, 0)
     right_side(0)
     mix(w0, 1)
+    right_side(1, range(3))
     s1, s2 = exchange_finish(1, started, 2)
 
     def inverse(x):
@@ -322,8 +326,8 @@
     n11 = r0 * i0 * i0
     n01 = (v0w0 - a0 * n00) * i0
 
-    k_image, k_w0 = row(i0), row(a0 * i0)
-    right_side(1)
+    k_image, k_w0 = row(i0 * i0), row(a0 * i0 * i0)
+    right_side(1, range(3, 5))
 
     def finish1(s, p, image):
         before = w0[s, p].astype(f32)
@@ -332,44 +336,45 @@
         return value * u[s, p].astype(f32), value * before, value * value
 
     started = exchange_start(2, left_side(finish1, 3))
-    mix(w1, 0)
-    right_side(0)
-    mix(w1, 1)
+    for s in range(nsec):
+        mix(w1, s)
+        right_side(s)
+
+    def finish2(s, p, image):
+        w2[s, p] = image.astype(bf16)
+        older, before = w0[s, p].astype(f32), w1[s, p].astype(f32)
+        return image * u[s, p].astype(f32), image * older, image * before, image * image
+
+    last = exchange_start(3, left_side(finish2, 4))
     d0, d1, d2 = exchange_finish(2, started, 3)
-    v0w1 = c0 * d0
-    v1w1 = (d1 - a0 * v0w1) * i0
+    v0w1 = c0 * d0 * b0
+    v1w1 = d1 - a0 * c0 * d0
+    w1w1 = d2 * b0 * b0
     a1 = v1w1 * inv_count
-    r1 = d2 + a1 * a1 * n11 + b0 * b0 * n00 - 2.0 * a1 * v1w1 - 2.0 * b0 * v0w1 + 2.0 * a1 * b0 * n01
+    r1 = w1w1 + a1 * a1 * n11 + b0 * b0 * n00 - 2.0 * a1 * v1w1 - 2.0 * b0 * v0w1 + 2.0 * a1 * b0 * n01
     b1 = root(r1)
     i1 = inverse(b1)
     n22 = r1 * i1 * i1
     n12 = (v1w1 - a1 * n11 - b0 * n01) * i1
-
-    k_image2, k_w1, k_w02 = row(i1), row(a1 * i1), row(b0 * i1)
-    right_side(1)
-
-    def finish2(s, p, image):
-        older, before = w0[s, p].astype(f32), w1[s, p].astype(f32)
-        value = image * k_image2 - before * k_w1 - older * k_w02
-        w2[s, p] = value.astype(bf16)
-        return value * u[s, p].astype(f32), value * older, value * before, value * value
-
-    started = exchange_start(3, left_side(finish2, 4))
-    f0, f1, f2, f3 = exchange_finish(3, started, 4)
-    v0w2 = c0 * f0
-    v1w2 = (f1 - a0 * v0w2) * i0
-    v2w2 = (f2 - a1 * v1w2 - b0 * v0w2) * i1
+    ratio = b0 * i1
+    f0, f1, f2, f3 = exchange_finish(3, last, 4)
+    v0w2 = c0 * ratio * (f0 - a1 * d0 - s1)
+    v1w2 = (ratio * (f1 - a1 * d1 - s2) - a0 * v0w2) * i0
+    w1w2 = b0 * ratio * (f2 - a1 * d2 - d1)
+    w2w2 = ratio * ratio * (f3 + a1 * a1 * d2 + s2 - 2.0 * a1 * f2 - 2.0 * f1 + 2.0 * a1 * d1)
+    v2w2 = (w1w2 - a1 * v1w2 - b0 * v0w2) * i1
     a2 = v2w2 * inv_count
-    r2 = f3 + a2 * a2 * n22 + b1 * b1 * n11 - 2.0 * a2 * v2w2 - 2.0 * b1 * v1w2 + 2.0 * a2 * b1 * n12
+    r2 = w2w2 + a2 * a2 * n22 + b1 * b1 * n11 - 2.0 * a2 * v2w2 - 2.0 * b1 * v1w2 + 2.0 * a2 * b1 * n12
     b2 = root(r2)
     k3 = ritz[0, 3] / b2
     m2 = ritz[0, 2] - k3 * a2
     m1 = ritz[0, 1] - k3 * b1 - m2 * a1 * i1
     m0 = ritz[0, 0] - m2 * b0 * i1 - m1 * a0 * i0
+    k_last = k3 * ratio
     lane = lax.broadcasted_iota(jnp.int32, (1, 128), 1)
     for i, (x, y0, y1) in enumerate(((a0, a1, a2), (b0, b1, b2))):
         tri_out[i : i + 1, :] = jnp.where(lane == 0, x, jnp.where(lane == 1, y0, y1))
-    for i, x in enumerate((m0 * c0, m1 * i0, m2 * i1, k3)):
+    for i, x in enumerate((m0 * c0, m1 * i0 - k_last, m2 * ratio - k_last * a1, k_last)):
         coef_out[i : i + 1, :] = row(x)
     for copy in pending:
         copy.wait_send()
@@ -421,8 +426,8 @@
             pltpu.VMEM((nsec, n, n), f32),
             pltpu.VMEM((nsec, 2, nstate, n, n), bf16),
             pltpu.VMEM((nsec, nstate, 2 * n, n), bf16),
-            pltpu.VMEM((4, 4, 8, 128), f32),
-            pltpu.VMEM((4, peers, 4, 8, 128), f32),
+            pltpu.VMEM((4, 8, 128), f32),
+            pltpu.VMEM((4, peers, 8, 128), f32),
             pltpu.VMEM((nsec, n, n), f32),
             pltpu.VMEM((nsec, 2, n, n), bf16),
             dma((4,)), dma((nsec, 6)), dma((nsec, 6)), dma((nsec, 6)), dma((nsec, 6)),

time: 66.2 us -> 63.3 us (0.956)
  Pallas kernels: 65.2 us -> 62.3 us
    pallas_call x1, Pallas kernels: 60.2 us -> 57.3 us  [on_device(): pl.pallas_call(kernel, out_shape=(field, field, field, field, pltpu.VMEM(...]
where the time goes in v3:
time: 63.3 us; the launch traced here: 63.1 us
  Pallas kernels  62.3 us (98%)
  between operations  0.82 us (1%)
    pallas_call x1, Pallas kernels, on_device(): pl.pallas_call(kernel, out_shape=(field, field, field, field, pltpu.VMEM(...  57.3 us
    pallas_call x1, Pallas kernels, on_device(): pl.pallas_call(combine, out_shape=(jax.ShapeDtypeStruct((total, n), f32),...  5.03 us

profile of v3, /device:TPU:1, one launch (start us, length us, event | category | flops | bytes accessed | tf_op | source)
XLA Modules:
  0.0 63.1 jit_solution(11240169974477374736)
XLA Ops:
  0.6 57.3 %shard_map.95 = (bf16[2,16,256,256]{3,2,1,0:T(8,128)(2,1)S(1)}, bf16[2,16,256,256]{3,2,1,0:T(8,128)(2,1)S(1)}, bf16[2,16,256,256]{3,2,1,0:T(8,128)(2,1)S(1)}, bf...) custom-call(s32[2]{0:T(128)} %sizes.1, s32[2,2]{1,0:T(2,128)} %gates.1, ...), custom_call_target="tpu_custom_call" | custom-call | tf_op jit(solution)/shard_map/pallas_call | solution.py:416
  57.9 5.0 %shard_map.96 = (f32[8192,256]{1,0:T(8,128)}, f32[1,2,3]{2,1,0:T(2,128)}) custom-call(f32[8,256]{1,0:T(8,128)S(1)} %get-tuple-element.10.coef, f32[8,128]{1,0:T(8,128)S(1)} %get-tuple-element.11.tri, bf16[8192,256]{1,0:T(8,128)(2,1)S(1)} %bitcast.6, bf16[8192,256]{1,0:T(8,128)(2,1)S(1)} %bitcast.7, bf16[8192,256]{1,0:T(8,128)(2,1)S(1)} %bitcast.8, ...), custom_call_target="tpu_custom_call" | custom-call | tf_op jit(solution)/shard_map/pallas_call | solution.py:446

commit v4 on v3

--- a/solution.py
+++ b/solution.py
@@ -150,15 +150,25 @@
         sums = jnp.sum(total, axis=1, keepdims=True)
         return [sums[i : i + 1] for i in range(amount)]
 
-    def mix(src, s):
+    mid = nstate - 2
+
+    def mix(load, s):
         def step(i, _):
             span = pl.ds(pl.multiple_of(i * 16, 16), 16)
-            block = src[s, :, span, :].reshape(nstate * 16, n)
-            out = mm(wk[...], block).astype(bf16).reshape(2, nstate, 16, n)
-            mixed[s, :, :, span, :] = out
+            block = load(s, slice(None), span).reshape(nstate * 16, n)
+            out = mm(wk[...], block).astype(bf16).reshape(2, mid, 16, n)
+            mixed[s, :, 1 : nstate - 1, span, :] = out
             return 0
 
         lax.fori_loop(0, n // 16, step, 0, unroll=True)
+        for p in (0, nstate - 1):
+            alone = load(s, p, slice(None)).astype(f32)
+            for w in range(2):
+                q = w * nstate + p
+                mixed[s, w, p] = (alone * weights[q : q + 1, p : p + 1]).astype(bf16)
+
+    def plain(ref):
+        return lambda s, states, span: ref[s, states, span, :]
 
     def right_side(s, levels=range(5)):
         for level in levels:
@@ -203,10 +213,10 @@
     state_row = lax.broadcasted_iota(jnp.int32, shape, 0) % nstate
     state_col = lax.broadcasted_iota(jnp.int32, shape, 1)
     table = jnp.where(charge(state_row) == charge(state_col), weights[...], 0.0).astype(bf16)
-    tall = (2 * nstate * 16, 2 * nstate)
-    spread_rows = jnp.where(
-        lax.broadcasted_iota(jnp.int32, tall, 0) // 16 == lax.broadcasted_iota(jnp.int32, tall, 1), 1.0, 0.0
-    ).astype(bf16)
+    tall = (2 * mid * 16, 2 * nstate)
+    which = lax.broadcasted_iota(jnp.int32, tall, 0) // 16
+    which = which + jnp.where(which < mid, 1, 3)
+    spread_rows = jnp.where(which == lax.broadcasted_iota(jnp.int32, tall, 1), 1.0, 0.0).astype(bf16)
     wide = (nstate, nstate * 16)
     spread_cols = jnp.where(
         lax.broadcasted_iota(jnp.int32, wide, 1) // 16 == lax.broadcasted_iota(jnp.int32, wide, 0), 1.0, 0.0
@@ -232,7 +242,7 @@
     started = exchange_start(0, [square])
     for s in range(nsec):
         line_forward(copies[s], gbuf, s, *ring_y)
-        mix(u, s)
+        mix(plain(u), s)
 
     def slot(buf, at, j, s):
         return decode(buf.at[lax.rem(at - j + LINE, LINE), s])
@@ -305,9 +315,9 @@
             env[s, :, w * n : (w + 1) * n] = left.astype(bf16)
         sums = left_of(finish0, s, sums)
     started = exchange_start(1, sums)
-    mix(w0, 0)
+    mix(plain(w0), 0)
     right_side(0)
-    mix(w0, 1)
+    mix(plain(w0), 1)
     right_side(1, range(3))
     s1, s2 = exchange_finish(1, started, 2)
 
@@ -326,18 +336,23 @@
     n11 = r0 * i0 * i0
     n01 = (v0w0 - a0 * n00) * i0
 
-    k_image, k_w0 = row(i0 * i0), row(a0 * i0 * i0)
+    shift = a0 * i0 * i0
+    k_image, k_w0 = row(i0 * i0), row(shift)
     right_side(1, range(3, 5))
 
     def finish1(s, p, image):
         before = w0[s, p].astype(f32)
-        value = image * k_image - before * k_w0
+        value = image * k_image
         w1[s, p] = value.astype(bf16)
         return value * u[s, p].astype(f32), value * before, value * value
 
     started = exchange_start(2, left_side(finish1, 3))
-    for s in range(nsec):
-        mix(w1, s)
+    def shifted(s, states, span):
+        value = w1[s, states, span, :].astype(f32) - w0[s, states, span, :].astype(f32) * k_w0
+        return value.astype(bf16)
+
+    for s in range(nsec):
+        mix(shifted, s)
         right_side(s)
 
     def finish2(s, p, image):
@@ -346,7 +361,10 @@
         return image * u[s, p].astype(f32), image * older, image * before, image * image
 
     last = exchange_start(3, left_side(finish2, 4))
-    d0, d1, d2 = exchange_finish(2, started, 3)
+    d0, e1, d2 = exchange_finish(2, started, 3)
+    d0 = d0 - shift * s1
+    d1 = e1 - shift * s2
+    d2 = d2 - 2.0 * shift * e1 + shift * shift * s2
     v0w1 = c0 * d0 * b0
     v1w1 = d1 - a0 * c0 * d0
     w1w1 = d2 * b0 * b0
@@ -358,6 +376,7 @@
     n12 = (v1w1 - a1 * n11 - b0 * n01) * i1
     ratio = b0 * i1
     f0, f1, f2, f3 = exchange_finish(3, last, 4)
+    f2 = f2 - shift * f1
     v0w2 = c0 * ratio * (f0 - a1 * d0 - s1)
     v1w2 = (ratio * (f1 - a1 * d1 - s2) - a0 * v0w2) * i0
     w1w2 = b0 * ratio * (f2 - a1 * d2 - d1)
@@ -371,10 +390,11 @@
     m1 = ritz[0, 1] - k3 * b1 - m2 * a1 * i1
     m0 = ritz[0, 0] - m2 * b0 * i1 - m1 * a0 * i0
     k_last = k3 * ratio
+    k_next = m2 * ratio - k_last * a1
     lane = lax.broadcasted_iota(jnp.int32, (1, 128), 1)
     for i, (x, y0, y1) in enumerate(((a0, a1, a2), (b0, b1, b2))):
         tri_out[i : i + 1, :] = jnp.where(lane == 0, x, jnp.where(lane == 1, y0, y1))
-    for i, x in enumerate((m0 * c0, m1 * i0 - k_last, m2 * ratio - k_last * a1, k_last)):
+    for i, x in enumerate((m0 * c0, m1 * i0 - k_last - k_next * shift, k_next, k_last)):
         coef_out[i : i + 1, :] = row(x)
     for copy in pending:
         copy.wait_send()
@@ -421,7 +441,7 @@
         scratch_shapes=[
             code, code,
             pltpu.VMEM((nsec + 4, 2, n, n), bf16),
-            pltpu.VMEM((2 * nstate * 16, nstate * 16), bf16),
+            pltpu.VMEM((2 * (nstate - 2) * 16, nstate * 16), bf16),
             pltpu.VMEM((nsec, n, 2 * n), bf16),
             pltpu.VMEM((nsec, n, n), f32),
             pltpu.VMEM((nsec, 2, nstate, n, n), bf16),

time: 63.3 us -> 62.5 us (0.987)
  Pallas kernels: 62.3 us -> 61.5 us
    pallas_call x1, Pallas kernels: 57.3 us -> 56.5 us  [on_device(): pl.pallas_call(kernel, out_shape=(field, field, field, field, pltpu.VMEM(...]
where the time goes in v4:
time: 62.5 us; the launch traced here: 62.3 us
  Pallas kernels  61.5 us (98%)
  between operations  0.82 us (1%)
    pallas_call x1, Pallas kernels, on_device(): pl.pallas_call(kernel, out_shape=(field, field, field, field, pltpu.VMEM(...  56.5 us
    pallas_call x1, Pallas kernels, on_device(): pl.pallas_call(combine, out_shape=(jax.ShapeDtypeStruct((total, n), f32),...  5.03 us

profile of v4, /device:TPU:1, one launch (start us, length us, event | category | flops | bytes accessed | tf_op | source)
XLA Modules:
  0.0 62.3 jit_solution(15804540558268627704)
XLA Ops:
  0.6 56.5 %shard_map.95 = (bf16[2,16,256,256]{3,2,1,0:T(8,128)(2,1)S(1)}, bf16[2,16,256,256]{3,2,1,0:T(8,128)(2,1)S(1)}, bf16[2,16,256,256]{3,2,1,0:T(8,128)(2,1)S(1)}, bf...) custom-call(s32[2]{0:T(128)} %sizes.1, s32[2,2]{1,0:T(2,128)} %gates.1, ...), custom_call_target="tpu_custom_call" | custom-call | tf_op jit(solution)/shard_map/pallas_call | solution.py:436
  57.1 5.0 %shard_map.96 = (f32[8192,256]{1,0:T(8,128)}, f32[1,2,3]{2,1,0:T(2,128)}) custom-call(f32[8,256]{1,0:T(8,128)S(1)} %get-tuple-element.10.coef, f32[8,128]{1,0:T(8,128)S(1)} %get-tuple-element.11.tri, bf16[8192,256]{1,0:T(8,128)(2,1)S(1)} %bitcast.6, bf16[8192,256]{1,0:T(8,128)(2,1)S(1)} %bitcast.7, bf16[8192,256]{1,0:T(8,128)(2,1)S(1)} %bitcast.8, ...), custom_call_target="tpu_custom_call" | custom-call | tf_op jit(solution)/shard_map/pallas_call | solution.py:466

commit v5 on v4

--- a/solution.py
+++ b/solution.py
@@ -135,7 +135,7 @@
         ex_src[e] = tile
         copies = [
             remote(ex_src.at[e], ex_dst.at[e, sector], e_send.at[e, d], e_recv.at[e, d], on_sector(d))
-            for d in range(1, peers)
+            for d in sorted(range(1, peers), key=lambda d: -min(d, peers - d))
         ]
         ex_dst[e, sector] = tile
         pending.extend(copies)
@@ -361,6 +361,8 @@
         return image * u[s, p].astype(f32), image * older, image * before, image * image
 
     last = exchange_start(3, left_side(finish2, 4))
+    for copy in pending[: -len(last)]:
+        copy.wait_send()
     d0, e1, d2 = exchange_finish(2, started, 3)
     d0 = d0 - shift * s1
     d1 = e1 - shift * s2
@@ -396,7 +398,7 @@
         tri_out[i : i + 1, :] = jnp.where(lane == 0, x, jnp.where(lane == 1, y0, y1))
     for i, x in enumerate((m0 * c0, m1 * i0 - k_last - k_next * shift, k_next, k_last)):
         coef_out[i : i + 1, :] = row(x)
-    for copy in pending:
+    for copy in last:
         copy.wait_send()
 
 
@@ -462,7 +464,7 @@
     )
     total = nsec * nstate * n
     flat = [x.reshape(total, n) for x in (u, w0, w1, w2)]
-    parts = 16
+    parts = 32
     psi, tridiag = pl.pallas_call(
         combine,
         out_shape=(jax.ShapeDtypeStruct((total, n), f32), jax.ShapeDtypeStruct((1, 2, 3), f32)),

time: 62.5 us -> 61.9 us (level)
  no operation moved by 1% of the time
where the time goes in v5:
time: 61.9 us; the launch traced here: 61.7 us
  Pallas kernels  60.9 us (98%)
  between operations  0.82 us (1%)
    pallas_call x1, Pallas kernels, on_device(): pl.pallas_call(kernel, out_shape=(field, field, field, field, pltpu.VMEM(...  56.3 us
    pallas_call x1, Pallas kernels, on_device(): pl.pallas_call(combine, out_shape=(jax.ShapeDtypeStruct((total, n), f32),...  4.54 us

profile of v5, /device:TPU:1, one launch (start us, length us, event | category | flops | bytes accessed | tf_op | source)
XLA Modules:
  0.0 61.7 jit_solution(4117221225635684301)
XLA Ops:
  0.6 56.3 %shard_map.95 = (bf16[2,16,256,256]{3,2,1,0:T(8,128)(2,1)S(1)}, bf16[2,16,256,256]{3,2,1,0:T(8,128)(2,1)S(1)}, bf16[2,16,256,256]{3,2,1,0:T(8,128)(2,1)S(1)}, bf...) custom-call(s32[2]{0:T(128)} %sizes.1, s32[2,2]{1,0:T(2,128)} %gates.1, ...), custom_call_target="tpu_custom_call" | custom-call | tf_op jit(solution)/shard_map/pallas_call | solution.py:438
  57.0 4.5 %shard_map.96 = (f32[8192,256]{1,0:T(8,128)}, f32[1,2,3]{2,1,0:T(2,128)}) custom-call(f32[8,256]{1,0:T(8,128)S(1)} %get-tuple-element.10.coef, f32[8,128]{1,0:T(8,128)S(1)} %get-tuple-element.11.tri, bf16[8192,256]{1,0:T(8,128)(2,1)S(1)} %bitcast.6, bf16[8192,256]{1,0:T(8,128)(2,1)S(1)} %bitcast.7, bf16[8192,256]{1,0:T(8,128)(2,1)S(1)} %bitcast.8, ...), custom_call_target="tpu_custom_call" | custom-call | tf_op jit(solution)/shard_map/pallas_call | solution.py:468
